TPU v7x, 768 devices: a whole 4x8x12 slice. The times are simulated.
768 devices in a mesh: branch: 12 (over x, z_hi), shard: 64 (over z_lo, y, core).
Axes of the slice: x: 4, y: 8, z: 12 (z_hi: 3, z_lo: 4; z = z_hi * 4 + z_lo), core: 2. Of those that a mesh axis runs over, the one named last changes fastest.
Arguments:
- resid: bfloat16 [2304, 4096], P('branch', 'shard'), may hold values from -6 to 6
- context: bfloat16 [2304, 4096], P('branch'), may hold values from -6 to 6
- o_weight: bfloat16 [12, 4096, 4096], P('branch', None, 'shard'), may hold values from -0.3125 to 0.3125
- gain: bfloat16 [4096], replicated, may hold values from 0.099609375 to 1.8984375
- expert_ids: int32 [2304, 2], P('branch'), may hold values from 0 to 11, all different within a row; in each aligned block of 192 rows (0 to 191, 192 to 383, ...) at most 40 rows name the same one
- combine_codes: int32 [2304, 2], P('branch'), may hold values from 1 to 63
- gate_weight: bfloat16 [12, 4096, 8192], P('branch', None, 'shard'), may hold values from -0.09375 to 0.09375
- up_weight: bfloat16 [12, 4096, 8192], P('branch', None, 'shard'), may hold values from -0.09375 to 0.09375
- down_weight: bfloat16 [12, 8192, 4096], P('branch', 'shard'), may hold values from -0.1875 to 0.1875
Outputs:
- mixed: bfloat16 [2304, 4096], P('branch', 'shard')
- merged_weight: bfloat16 [4096, 4096], P(None, 'shard')
Inputs may be any that keep to these rules, and one draw needn't show every extreme that they name: `expert_ids`: each token names two different experts. Among the 192 tokens of one branch no expert is named more than 40 times, a bound that some block reaches.
All inputs are finite; a program needn't handle non-finite values.
Results may differ from a plain program's by a relative error of at most 0.022.
Values may be sent and summed in bfloat16 or wider, within the bound.
No kernel may reach another device: no remote copies, remote signals or barrier semaphores. Data moves between devices by JAX's collectives and lax.ppermute only.
A program may use at most 64 MiB of HBM per device.

v0:
```python
import jax
import jax.numpy as jnp
from jax import lax
from jax.sharding import PartitionSpec as P

epsilon = 1e-05


def slot_index(route_rows, n_experts, capacity):
    flat_ids = route_rows.reshape(-1)
    onehot = (flat_ids[:, None] == jnp.arange(n_experts, dtype=jnp.int32)[None, :]).astype(
        jnp.int32
    )
    before = jnp.cumsum(onehot, axis=0) - onehot
    position = jnp.sum(before * onehot, axis=1)
    return flat_ids * capacity + position


def local(
    resid, context, o_weight, gain, expert_ids, combine_codes, gate_weight, up_weight, down_weight
):
    n_experts = lax.axis_size("branch")
    tok_rows = resid.shape[0]
    feat_width = resid.shape[1]
    full_width = context.shape[1]
    capacity = 5 * tok_rows // (2 * n_experts)
    slot_rows = n_experts * capacity
    summed = lax.psum(o_weight[0].astype(jnp.float32).astype(jnp.bfloat16), "branch").astype(
        jnp.float32
    )
    merged = (summed / n_experts).astype(jnp.bfloat16)
    hidden_state = (
        resid.astype(jnp.float32) + jnp.dot(context, merged, preferred_element_type=jnp.float32)
    ).astype(jnp.bfloat16)
    state_f = hidden_state.astype(jnp.float32)
    slots = slot_index(expert_ids, n_experts, capacity)
    pick_table = (slots[None, :] == jnp.arange(slot_rows, dtype=jnp.int32)[:, None]).astype(
        jnp.bfloat16
    )
    offset = lax.axis_index("shard") * feat_width
    squares = lax.psum(jnp.sum(state_f * state_f, axis=1), "shard")
    inv_scale = lax.rsqrt(squares / full_width + epsilon)
    gain_part = lax.dynamic_slice_in_dim(gain, offset, feat_width).astype(jnp.float32)
    moving = (state_f * inv_scale[:, None] * gain_part[None, :]).astype(jnp.bfloat16)
    repeated = jnp.repeat(moving, 2, axis=0)
    sent_rows = jnp.dot(pick_table, repeated, preferred_element_type=jnp.float32).astype(
        jnp.bfloat16
    )
    sent_rows = sent_rows.reshape(n_experts, capacity, feat_width)
    arrived = lax.all_to_all(sent_rows, "branch", split_axis=0, concat_axis=0, tiled=True).reshape(
        slot_rows, feat_width
    )
    w_gate = gate_weight[0]
    w_up = up_weight[0]
    block_rows = lax.all_gather(arrived, "shard", axis=1, tiled=True)
    gate_acts = jnp.dot(block_rows, w_gate, preferred_element_type=jnp.float32)
    up_acts = jnp.dot(block_rows, w_up, preferred_element_type=jnp.float32)
    inner = (jax.nn.silu(gate_acts) * up_acts).astype(jnp.bfloat16)
    partial_value = jnp.dot(inner, down_weight[0], preferred_element_type=jnp.float32)
    expert_out = lax.psum_scatter(partial_value, "shard", scatter_dimension=1, tiled=True).astype(
        jnp.bfloat16
    )
    expert_out = expert_out.reshape(n_experts, capacity, feat_width)
    returned = lax.all_to_all(
        expert_out, "branch", split_axis=0, concat_axis=0, tiled=True
    ).reshape(slot_rows, feat_width)
    picked = jnp.einsum("mr,md->rd", pick_table, returned, preferred_element_type=jnp.float32)
    picked = picked.reshape(tok_rows, 2, feat_width)
    code_vals = combine_codes.astype(jnp.float32)
    mix_weights = code_vals / jnp.sum(code_vals, axis=1, keepdims=True)
    mixture = jnp.sum(picked * mix_weights[:, :, None], axis=1)
    mixed = (state_f + mixture).astype(jnp.bfloat16)
    return (mixed, merged)


def solution(mesh):
    in_specs = (
        P("branch", "shard"),
        P("branch", None),
        P("branch", None, "shard"),
        P(),
        P("branch", None),
        P("branch", None),
        P("branch", None, "shard"),
        P("branch", None, "shard"),
        P("branch", "shard", None),
    )
    out_specs = (P("branch", "shard"), P(None, "shard"))
    return jax.shard_map(local, mesh=mesh, in_specs=in_specs, out_specs=out_specs, check_vma=False)
```

profile of v0, /device:TPU:1, one launch (start us, length us, event | category | flops | bytes accessed | tf_op | source)
XLA Modules:
  0.0 780.1 jit_solution(6865783809114913844)
XLA Ops:
  7.2 0.7 all-reduce.2.cloned.1.call-update
  8.0 0.8 copy.33
  8.8 0.1 eq.58
  8.9 0.9 reduce-window.6
  9.8 0.2 slice_reduce_fusion
  10.1 0.1 reshape.70
  10.3 0.8 dynamic-slice_convert_fusion
  11.1 164.7 %all-reduce.2.cloned.1.call-done = bf16[4096,64]{0,1:T(8,128)(2,1)} async-done(((bf16[4096,64]{0,1:T(8,128)(2,1)}), bf16[4096,64]{0,1:T(8,128)(2,1)}) %all-reduce.2.cloned.1.call-update) | async-done | bytes 524304 | tf_op jit(solution)/shard_map/psum | solution.py:28
  175.8 1.1 multiply_convert_fusion
  177.0 1.5 multiply_reduce_fusion
  178.5 140.8 %psum.15 = f32[192]{0:T(256)S(1)} all-reduce(f32[192]{0:T(256)S(1)} %get-tuple-element.2), channel_id=1, replica_groups=mesh['branch'=12,'shard'=64] {'shard'}, use_global_device_ids=true, to_apply=%region_5.6 | all-reduce | flops 192 | bytes 1536 | tf_op jit(solution)/shard_map/psum | solution.py:41
  319.4 0.1 copy.37
  319.6 0.3 convolution_convert_fusion
  319.9 0.1 copy.38
  320.1 0.1 reshape.79
  320.2 14.5 %all_to_all.10 = bf16[12,2,1280]{2,1,0:T(2,128)(2,1)S(1)} all-to-all(bf16[12,2,1280]{2,1,0:T(2,128)(2,1)S(1)} %reshape.79), channel_id=1, replica_groups=mesh['branch'=12,'shard'=64] {'branch'}, dimensions={0} | all-to-all | bytes 122880 | tf_op jit(solution)/shard_map/all_to_all | solution.py:50
  334.7 0.1 reshape.80
  334.8 0.7 copy.39
  335.6 113.5 %all-gather.2.cloned.1.call-done = bf16[480,4096]{0,1:T(8,128)(2,1)} async-done(((bf16[480,64]{0,1:T(8,128)(2,1)}), bf16[480,4096]{0,1:T(8,128)(2,1)}) %all-gather.2.cloned.1.call-update) | async-done | bytes 3932176 | tf_op jit(solution)/shard_map/all_gather | solution.py:55
  449.1 3.8 fusion.9
  452.9 10.1 %fusion.1 = f32[480,4096]{0,1:T(8,128)} fusion(bf16[480,4096]{0,1:T(8,128)(2,1)} %all-gather.2.cloned.1.call-done, bf16[1,128,4096]{2,1,0:T(8,128)(2,1)S(1)} %copy-done.2, bf16[1,4096,128]{2,1,0:T(8,128)(2,1)} %param.16, f32[480,128]{1,0:T(8,128)S(1)} %fusion.9), kind=kOutput, calls=%fused_computation.3 | convolution fusion | flops 1007001600 | bytes 14139392 | tf_op jit(solution)/shard_map/dot_general | solution.py:59
  463.0 0.1 reduce_sum.39
  463.2 0.4 copy-done.4
  463.7 289.5 %reduce-scatter.2.cloned.1.call-done = f32[480,64]{0,1:T(8,128)} async-done(((f32[480,4096]{0,1:T(8,128)}), f32[480,64]{0,1:T(8,128)}) %reduce-scatter.2.cloned.1.call-update) | async-done | bytes 122896 | tf_op jit(solution)/shard_map/reduce_scatter | solution.py:60
  753.1 0.9 convert_element_type.57
  754.1 0.1 copy.40
  754.2 0.8 reshape.81
  755.0 8.2 %all-to-all-start.1 = ((bf16[12,2,1280]{2,1,0:T(2,128)(2,1)}), bf16[12,2,1280]{2,1,0:T(2,128)(2,1)S(1)}, u32[]{:S(2)}, u32[]{:S(2)}) async-start(bf16[12,2,1280]{2,1,0:T(2,128)(2,1)} %reshape.81), calls=%async_computation.2 | async-start | bytes 122880 | tf_op jit(solution)/shard_map/all_to_all | solution.py:64
  763.2 9.2 %all-to-all-done.1 = bf16[12,2,1280]{2,1,0:T(2,128)(2,1)S(1)} async-done(((bf16[12,2,1280]{2,1,0:T(2,128)(2,1)}), bf16[12,2,1280]{2,1,0:T(2,128)(2,1)S(1)}, u32[]{:S(2)}, u32[]{:S(2)}) %all-to-all-start.1) | async-done | bytes 61472 | tf_op jit(solution)/shard_map/all_to_all | solution.py:64
  772.4 0.1 reshape.82
  772.6 0.4 fusion.2
  773.0 0.6 add_convert_fusion
  (29 shorter events, 0.6 us)
Async XLA Ops:
  7.2 169.8 %copy-start = (bf16[192,4096]{1,0:T(8,128)(2,1)S(1)}, bf16[192,4096]{1,0:T(8,128)(2,1)}, u32[]{:S(2)}) copy-start(bf16[192,4096]{1,0:T(8,128)(2,1)} %param.10) | copy-start | bytes 4718596
  7.2 168.7 %all-reduce.2.cloned.1.call-start = ((), (), s32[]{:S(2)}) async-start(), calls=%async_computation.3 | async-start | bytes 1048576 | tf_op jit(solution)/shard_map/psum | solution.py:28
  7.9 441.2 %all-gather.2.cloned.1.call-start = ((), (), s32[]{:S(2)}) async-start(), calls=%async_computation.4 | async-start | bytes 4259840 | tf_op jit(solution)/shard_map/all_gather | solution.py:55
  177.0 275.9 %copy-start.1 = (bf16[4096,64]{0,1:T(8,128)(2,1)}, bf16[4096,64]{0,1:T(8,128)(2,1)S(1)}, u32[]{:S(2)}) copy-start(bf16[4096,64]{0,1:T(8,128)(2,1)S(1)} %multiply_convert_fusion) | copy-start | bytes 1572868
  177.0 275.9 %copy-start.2 = (bf16[1,128,4096]{2,1,0:T(8,128)(2,1)S(1)}, bf16[1,128,4096]{2,1,0:T(8,128)(2,1)}, u32[]{:S(2)}) copy-start(bf16[1,128,4096]{2,1,0:T(8,128)(2,1)} %param.17) | copy-start | bytes 3145732
  335.6 417.6 %reduce-scatter.2.cloned.1.call-start = ((), (), s32[]{:S(2)}) async-start(), calls=%async_computation.5 | async-start | bytes 8519680 | tf_op jit(solution)/shard_map/reduce_scatter | solution.py:60
  462.9 0.7 copy-start.4
  462.9 0.7 copy-start.3
  755.0 17.5 %all-to-all-start.1 = ((bf16[12,2,1280]{2,1,0:T(2,128)(2,1)}), bf16[12,2,1280]{2,1,0:T(2,128)(2,1)S(1)}, u32[]{:S(2)}, u32[]{:S(2)}) async-start(bf16[12,2,1280]{2,1,0:T(2,128)(2,1)} %reshape.81), calls=%async_computation.2 | async-start | bytes 122880 | tf_op jit(solution)/shard_map/all_to_all | solution.py:64
Sparse Core Ops, SparseCore 0:
  11.2 164.5 all-reduce.1
  335.7 113.3 all-gather.1
  463.1 290.0 reduce-scatter.1
where the time goes:
time: 785 us; the launch traced here: 780 us
  waiting for transfers between devices  578 us (74%)
  blocking collectives  155 us (20%)
  matrix products  16 us (2%)
  between operations  13.9 us (2%)
  starting transfers between devices  8.37 us (1%)
    reduce_scatter x1, waiting for transfers between devices, local(): lax.psum_scatter(partial_value, 'shard', scatter_dimension=1, tiled=True)  289 us
    psum x1, waiting for transfers between devices, local(): lax.psum(o_weight[0].astype(jnp.float32).astype(jnp.bfloat16), 'branch')  165 us
    psum x1, blocking collectives, local(): squares = lax.psum(jnp.sum(state_f * state_f, axis=1), 'shard')  141 us
    all_gather x1, waiting for transfers between devices, local(): block_rows = lax.all_gather(arrived, 'shard', axis=1, tiled=True)  113 us
  transfers between devices with their start and end apart: 4, of which 4 were waited for; matrix products, arithmetic and copies ran while one was open for 0% of the time, Pallas kernels for 0%

commit v1 on v0

v1 whole, which is shorter than its diff:
```python
import jax
import jax.numpy as jnp
from jax import lax
from jax.experimental import pallas as pl
from jax.experimental.pallas import tpu as pltpu
from jax.sharding import Mesh, PartitionSpec as P

epsilon = 1e-05
MEMBERS = 4
RING = 8
SHARD = ("group", "chip", "core")
LANES = 128
BF16 = jnp.bfloat16
F32 = jnp.float32


def expert_kernel(x_ref, gain_ref, *refs):
    given, out_ref, rows_ref, weights, sems = refs[:MEMBERS], *refs[MEMBERS:]

    def fetch(m, kind):
        return pltpu.make_async_copy(given[m].at[kind], weights.at[m, kind], sems.at[m, kind])

    for m in range(MEMBERS):
        fetch(m, 0).start()
        fetch(m, 1).start()
    for m in range(MEMBERS):
        fetch(m, 2).start()
    sources, half, _ = x_ref.shape
    width = rows_ref.shape[1]
    low = lax.broadcasted_iota(jnp.int32, (half, LANES), 1) < LANES // 2
    squares = [jnp.zeros((half, LANES), F32), jnp.zeros((half, LANES), F32)]
    for q in range(sources // 2):
        even, odd = x_ref[2 * q].astype(F32), x_ref[2 * q + 1].astype(F32)
        top = jnp.where(low, even, pltpu.roll(odd, LANES // 2, 1))
        bottom = jnp.where(low, pltpu.roll(even, LANES // 2, 1), odd)
        squares[0] += top * top
        squares[1] += bottom * bottom
        rows_ref[:half, q * LANES : (q + 1) * LANES] = top.astype(BF16)
        rows_ref[half:, q * LANES : (q + 1) * LANES] = bottom.astype(BF16)
    total = jnp.sum(jnp.concatenate(squares, axis=0), axis=1, keepdims=True)
    inverse = lax.rsqrt(total / width + epsilon)
    chunk = 2 * LANES
    for k in range(0, width, chunk):
        gain = gain_ref[:, k : k + chunk]
        rows_ref[:, k : k + chunk] = (rows_ref[:, k : k + chunk].astype(F32) * inverse * gain).astype(BF16)
    inner = []
    for m in range(MEMBERS):
        fetch(m, 0).wait()
        fetch(m, 1).wait()
        acts = jnp.zeros((2 * half, 2 * LANES), F32)
        for k in range(0, width, chunk):
            both = jnp.concatenate([weights[m, 0, k : k + chunk, :], weights[m, 1, k : k + chunk, :]], axis=1)
            acts += jnp.dot(rows_ref[:, k : k + chunk], both, preferred_element_type=F32)
        gate_acts, up_acts = acts[:, :LANES], acts[:, LANES:]
        inner.append((gate_acts / (1.0 + jnp.exp(-gate_acts)) * up_acts).astype(BF16))
    inner = jnp.concatenate(inner, axis=1)
    for m in range(MEMBERS):
        fetch(m, 2).wait()
    for q in range(0, width // LANES, 2):
        columns = [
            jnp.concatenate([weights[m, 2, (q + j) * LANES : (q + j + 1) * LANES, :] for m in range(MEMBERS)], axis=0)
            for j in range(2)
        ]
        part = jnp.dot(inner, jnp.concatenate(columns, axis=1), preferred_element_type=F32)
        for j in range(2):
            s = 2 * (q + j)
            top = part[:half, j * LANES : (j + 1) * LANES]
            bottom = part[half:, j * LANES : (j + 1) * LANES]
            out_ref[s] = jnp.where(low, top, pltpu.roll(bottom, LANES // 2, 1)).astype(BF16)
            out_ref[s + 1] = jnp.where(low, pltpu.roll(top, LANES // 2, 1), bottom).astype(BF16)


def run_expert(x, gain, weights):
    sources, half, _ = x.shape
    width = gain.shape[1]
    size = sum(w.size for w in weights)
    return pl.pallas_call(
        expert_kernel,
        out_shape=jax.ShapeDtypeStruct(x.shape, BF16),
        in_specs=[pl.BlockSpec(memory_space=pltpu.VMEM)] * 2 + [pl.BlockSpec(memory_space=pl.ANY)] * MEMBERS,
        out_specs=pl.BlockSpec(memory_space=pltpu.VMEM),
        scratch_shapes=[
            pltpu.VMEM((2 * half, width), BF16),
            pltpu.VMEM((MEMBERS,) + weights[0].shape, BF16),
            pltpu.SemaphoreType.DMA((MEMBERS, 3)),
        ],
        compiler_params=pltpu.CompilerParams(vmem_limit_bytes=56 * 1024 * 1024),
        cost_estimate=pl.CostEstimate(
            flops=2 * 2 * half * size, bytes_accessed=2 * (2 * x.size + size), transcendentals=0
        ),
    )(x, gain, *weights)


def ring_pairs(shards):
    pairs = []
    for source in range(shards):
        line, place, core = source // (2 * RING), source // 2 % RING, source % 2
        step = 1 if place % 2 == core else RING - 1
        pairs.append((source, (line * RING + (place + step) % RING) * 2 + core))
    return pairs


def slot_index(route_rows, n_experts, capacity):
    flat_ids = route_rows.reshape(-1)
    count = flat_ids.shape[0]
    onehot = flat_ids[:, None] == jnp.arange(n_experts, dtype=jnp.int32)[None, :]
    order = jnp.arange(count, dtype=jnp.int32)
    earlier = (order[:, None] > order[None, :]).astype(BF16)
    before = jnp.dot(earlier, onehot.astype(BF16), preferred_element_type=F32)
    position = jnp.sum(jnp.where(onehot, before, 0.0), axis=1).astype(jnp.int32)
    return (flat_ids * capacity + position).reshape(route_rows.shape)


def local(
    resid, context, o_weight, gain, expert_ids, combine_codes, gate_weight, up_weight, down_weight
):
    n_experts = lax.axis_size("branch")
    n_groups = lax.axis_size("group")
    shards = n_groups * MEMBERS
    tok_rows, feat_width = resid.shape
    full_width = context.shape[1]
    capacity = 5 * tok_rows // (2 * n_experts)
    half_cap = capacity // 2
    quarter = n_experts // MEMBERS * half_cap
    half = -(-quarter // 16) * 16

    blocks = down_weight[0].reshape(-1, full_width // LANES, LANES).transpose(1, 0, 2).reshape(full_width, LANES)
    own = jnp.stack([gate_weight[0], up_weight[0], blocks])
    beside = lax.ppermute(own, SHARD, ring_pairs(shards))
    own_core = lax.ppermute(own, "core", [(0, 1), (1, 0)])

    piece = -(-full_width // (LANES * n_experts)) * LANES
    missing = n_experts * piece - full_width
    columns = jnp.pad(o_weight[0].T, ((0, 0), (0, missing))).reshape(feat_width, n_experts, piece)
    parts = lax.all_to_all(columns.transpose(1, 0, 2), "branch", 0, 0, tiled=True)
    mean_part = (jnp.sum(parts.astype(F32), axis=0) / n_experts).astype(BF16)
    spread = jnp.broadcast_to(mean_part[None], (n_experts, feat_width, piece))
    merged = lax.all_to_all(spread, "branch", 0, 0, tiled=True)
    merged = merged.transpose(1, 0, 2).reshape(feat_width, n_experts * piece)[:, :full_width].T

    hidden_state = (
        resid.astype(F32) + jnp.dot(context, merged, preferred_element_type=F32)
    ).astype(BF16)

    hidden_state, beside = lax.optimization_barrier((hidden_state, beside))
    beside_core = lax.ppermute(beside, "core", [(0, 1), (1, 0)])

    slots = slot_index(expert_ids, n_experts, capacity)
    all_slots = jnp.arange(n_experts * capacity, dtype=jnp.int32)
    pick_table = ((slots[None, :, 0] == all_slots[:, None]) | (slots[None, :, 1] == all_slots[:, None])).astype(BF16)
    sent = jnp.dot(pick_table, hidden_state, preferred_element_type=F32).astype(BF16)
    sent = sent.reshape(n_experts, 2, half_cap, feat_width)
    sent = jnp.concatenate([sent[:, 0], sent[:, 1]], axis=2)
    arrived = lax.all_to_all(sent, "branch", 0, 0, tiled=True)

    quarters = jnp.pad(arrived.reshape(MEMBERS, quarter, LANES), ((0, 0), (0, half - quarter), (0, 0)))
    copies = jnp.broadcast_to(quarters[None], (n_groups, MEMBERS, half, LANES)).reshape(shards, half, LANES)
    gathered = lax.all_to_all(copies, SHARD, 0, 0, tiled=True)
    partial_out = run_expert(gathered, gain.astype(F32).reshape(1, -1), (own, own_core, beside, beside_core))
    exchanged = lax.all_to_all(partial_out, SHARD, 0, 0, tiled=True)
    expert_out = jnp.sum(exchanged.reshape(n_groups, MEMBERS, half, LANES).astype(F32), axis=0).astype(BF16)

    expert_out = expert_out[:, :quarter].reshape(n_experts, half_cap, LANES)
    returned = lax.all_to_all(expert_out, "branch", 0, 0, tiled=True)
    returned = jnp.stack([returned[:, :, :feat_width], returned[:, :, feat_width:]], axis=1)
    returned = returned.reshape(n_experts * capacity, feat_width)
    code_vals = combine_codes.astype(F32)
    mix_weights = code_vals / jnp.sum(code_vals, axis=1, keepdims=True)
    mixture = jnp.zeros((tok_rows, feat_width), F32)
    for k in range(2):
        table = (slots[:, k, None] == all_slots[None, :]).astype(BF16)
        picked = jnp.dot(table, returned, preferred_element_type=F32)
        mixture += picked * mix_weights[:, k, None]
    mixed = (hidden_state.astype(F32) + mixture).astype(BF16)
    return (mixed, merged)


def solution(mesh):
    n_branches, n_shards = mesh.devices.shape
    fine = Mesh(mesh.devices.reshape(n_branches, n_shards // MEMBERS, 2, 2), ("branch",) + SHARD)
    in_specs = (
        P("branch", SHARD),
        P("branch", None),
        P("branch", None, SHARD),
        P(),
        P("branch", None),
        P("branch", None),
        P("branch", None, SHARD),
        P("branch", None, SHARD),
        P("branch", SHARD, None),
    )
    out_specs = (P("branch", SHARD), P(None, SHARD))
    return jax.shard_map(local, mesh=fine, in_specs=in_specs, out_specs=out_specs, check_vma=False)
```

time: 785 us -> 192 us (0.24)
  waiting for transfers between devices: 578 us -> 91.6 us
  blocking collectives: 155 us -> 0 us
  starting transfers between devices: 8.37 us -> 75.4 us
  matrix products: 16 us -> 2.25 us
  between operations: 13.9 us -> 0.96 us
    reduce_scatter x1 -> x0, waiting for transfers between devices: 289 us -> none  [local(): lax.psum_scatter(partial_value, 'shard', scatter_dimension=1, tiled=True)]
    psum x1 -> x0, waiting for transfers between devices: 165 us -> none  [local(): lax.psum(o_weight[0].astype(jnp.float32).astype(jnp.bfloat16), 'branch')]
    psum x1 -> x0, blocking collectives: 141 us -> none  [local(): squares = lax.psum(jnp.sum(state_f * state_f, axis=1), 'shard')]
    all_gather x1 -> x0, waiting for transfers between devices: 113 us -> none  [local(): block_rows = lax.all_gather(arrived, 'shard', axis=1, tiled=True)]
    all_to_all x1 -> x6, waiting for transfers between devices: 9.21 us -> 89.2 us  [the longest x1 28.6 us: local(): exchanged = lax.all_to_all(partial_out, SHARD, 0, 0, tiled=True)]
    all_to_all x1 -> x6, starting transfers between devices: 8.25 us -> 60.4 us  [the longest x1 17.3 us: local(): gathered = lax.all_to_all(copies, SHARD, 0, 0, tiled=True)]
    ppermute x0 -> x3, starting transfers between devices: none -> 15.1 us  [the longest x1 7.92 us: local(): own_core = lax.ppermute(own, 'core', [(0, 1), (1, 0)])]
    all_to_all x1 -> x0, blocking collectives: 14.5 us -> none  [local(): lax.all_to_all(sent_rows, 'branch', split_axis=0, concat_axis=0, tiled=True)]
  transfers between devices with their start and end apart: 4 -> 9, of which waited for: 4 -> 6; matrix products, arithmetic and copies ran while one was open for 0% -> 4% of each run, Pallas kernels for 0% -> 0%
where the time goes in v1:
time: 192 us; the launch traced here: 191 us
  waiting for transfers between devices  91.6 us (48%)
  starting transfers between devices  75.4 us (39%)
  local copies, waits for them, and re-layouts  9.72 us (5%)
  Pallas kernels  7.71 us (4%)
  other arithmetic  3.7 us (2%)
  matrix products  2.25 us (1%)
    all_to_all x1, waiting for transfers between devices, local(): exchanged = lax.all_to_all(partial_out, SHARD, 0, 0, tiled=True)  28.6 us
    all_to_all x1, waiting for transfers between devices, local(): gathered = lax.all_to_all(copies, SHARD, 0, 0, tiled=True)  28 us
    all_to_all x1, starting transfers between devices, local(): gathered = lax.all_to_all(copies, SHARD, 0, 0, tiled=True)  17.3 us
    all_to_all x1, starting transfers between devices, local(): lax.all_to_all(columns.transpose(1, 0, 2), 'branch', 0, 0, tiled=True)  17 us
    all_to_all x1, waiting for transfers between devices, local(): merged = lax.all_to_all(spread, 'branch', 0, 0, tiled=True)  12.6 us
    all_to_all x1, waiting for transfers between devices, local(): lax.all_to_all(columns.transpose(1, 0, 2), 'branch', 0, 0, tiled=True)  11.2 us
    all_to_all x1, starting transfers between devices, local(): arrived = lax.all_to_all(sent, 'branch', 0, 0, tiled=True)  9.05 us
    all_to_all x1, waiting for transfers between devices, local(): returned = lax.all_to_all(expert_out, 'branch', 0, 0, tiled=True)  8.89 us
  transfers between devices with their start and end apart: 9, of which 6 were waited for; matrix products, arithmetic and copies ran while one was open for 4% of the time, Pallas kernels for 0%

profile of v1, /device:TPU:1, one launch (start us, length us, event | category | flops | bytes accessed | tf_op | source)
XLA Modules:
  0.0 191.4 jit_solution(13593484498560636852)
XLA Ops:
  0.6 1.2 pad.8
  1.8 0.4 reshape.46
  2.3 0.9 copy.34
  3.2 17.0 %all-to-all-start = ((bf16[12,64,384]{2,1,0:T(8,128)(2,1)}), bf16[12,64,384]{2,1,0:T(8,128)(2,1)S(1)}, u32[]{:S(2)}, u32[]{:S(2)}) async-start(bf16[12,64,384]{2,1,0:T(8,128)(2,1)} %copy.34), calls=%async_computation | async-start | bytes 1179648 | tf_op jit(solution)/shard_map/all_to_all | solution.py:135
  20.5 0.4 copy.36
  20.9 0.5 copy-done.3
  21.4 0.3 copy-done.4
  21.7 2.0 %pad_maximum_fusion.refs_0_ = bf16[3,4096,128]{2,1,0:T(8,128)(2,1)} fusion(bf16[1,4096,128]{2,1,0:T(8,128)(2,1)S(1)} %bitcast.46, bf16[1,4096,128]{2,1,0:T(8,128)(2,1)S(1)} %copy-done.3, bf16[1,4096,128]{2,1,0:T(8,128)(2,1)S(1)} %copy-done.4), kind=kLoop, calls=%fused_computation | loop fusion | flops 3145728 | bytes 6291456 | tf_op jit(solution)/shard_map/stack | solution.py:128
  23.7 5.2 %collective-permute-start = (bf16[3,4096,128]{2,1,0:T(8,128)(2,1)}, bf16[3,4096,128]{2,1,0:T(8,128)(2,1)}, u32[]{:S(2)}, u32[]{:S(2)}) collective-permute-start(bf16[3,4096,128]{2,1,0:T(8,128)(2,1)} %pad_maximum_fusion.refs_0_), channel_id=1, source_target_pairs={{0,2},{1,15},{2,0},{3,5},{4,6},{5,3},{6,4},{7,9},{8,10},{9,7},{10,... | collective-permute-start | bytes 9437192 | tf_op jit(solution)/shard_map/ppermute | solution.py:129
  29.0 11.2 %all-to-all-done = bf16[12,64,384]{2,1,0:T(8,128)(2,1)S(1)} async-done(((bf16[12,64,384]{2,1,0:T(8,128)(2,1)}), bf16[12,64,384]{2,1,0:T(8,128)(2,1)S(1)}, u32[]{:S(2)}, u32[]{:S(2)}) %all-to-all-start) | async-done | bytes 589856 | tf_op jit(solution)/shard_map/all_to_all | solution.py:135
  40.2 0.9 broadcast_in_dim.7
  41.1 6.6 %all-to-all-start.1 = ((bf16[12,64,384]{2,1,0:T(8,128)(2,1)}), bf16[12,64,384]{2,1,0:T(8,128)(2,1)S(1)}, u32[]{:S(2)}, u32[]{:S(2)}) async-start(bf16[12,64,384]{2,1,0:T(8,128)(2,1)} %broadcast_in_dim.7), calls=%async_computation.1 | async-start | bytes 1179648 | tf_op jit(solution)/shard_map/all_to_all | solution.py:138
  48.4 12.6 %all-to-all-done.1 = bf16[12,64,384]{2,1,0:T(8,128)(2,1)S(1)} async-done(((bf16[12,64,384]{2,1,0:T(8,128)(2,1)}), bf16[12,64,384]{2,1,0:T(8,128)(2,1)S(1)}, u32[]{:S(2)}, u32[]{:S(2)}) %all-to-all-start.1) | async-done | bytes 589856 | tf_op jit(solution)/shard_map/all_to_all | solution.py:138
  61.1 0.6 fusion.2
  61.7 2.4 %collective-permute-done.refs_2_ = bf16[3,4096,128]{2,1,0:T(8,128)(2,1)} collective-permute-done((bf16[3,4096,128]{2,1,0:T(8,128)(2,1)}, bf16[3,4096,128]{2,1,0:T(8,128)(2,1)}, u32[]{:S(2)}, u32[]{:S(2)}) %collective-permute-start) | collective-permute-done | bytes 3145760 | tf_op jit(solution)/shard_map/ppermute | solution.py:129
  64.6 0.7 pad_maximum_fusion.2
  65.3 9.0 %all-to-all-start.2 = ((bf16[12,20,128]{2,1,0:T(8,128)(2,1)}), bf16[12,20,128]{2,1,0:T(8,128)(2,1)S(1)}, u32[]{:S(2)}, u32[]{:S(2)}) async-start(bf16[12,20,128]{2,1,0:T(8,128)(2,1)} %pad_maximum_fusion.2), calls=%async_computation.2 | async-start | bytes 147456 | tf_op jit(solution)/shard_map/all_to_all | solution.py:154
  74.4 7.9 %collective-permute-start.1 = (bf16[3,4096,128]{2,1,0:T(8,128)(2,1)}, bf16[3,4096,128]{2,1,0:T(8,128)(2,1)}, u32[]{:S(2)}, u32[]{:S(2)}) collective-permute-start(bf16[3,4096,128]{2,1,0:T(8,128)(2,1)} %pad_maximum_fusion.refs_0_), channel_id=1, source_target_pairs={{0,1},{1,0},{2,3},{3,2},{4,5},{5,4},{6,7},{7,6},{8,9},{9,8},{10,11... | collective-permute-start | bytes 9437192 | tf_op jit(solution)/shard_map/ppermute | solution.py:130
  82.3 1.9 %collective-permute-start.2 = (bf16[3,4096,128]{2,1,0:T(8,128)(2,1)}, bf16[3,4096,128]{2,1,0:T(8,128)(2,1)}, u32[]{:S(2)}, u32[]{:S(2)}) collective-permute-start(bf16[3,4096,128]{2,1,0:T(8,128)(2,1)} %collective-permute-done.refs_2_), channel_id=1, source_target_pairs={{0,1},{1,0},{2,3},{3,2},{4,5},{5,4},{6,7},{7,6},{8,9},{9,8},{10,11... | collective-permute-start | bytes 9437192 | tf_op jit(solution)/shard_map/ppermute | solution.py:146
  84.3 1.3 broadcast_in_dim.10
  85.6 17.3 %all-to-all-start.3 = ((bf16[64,64,128]{2,1,0:T(8,128)(2,1)}), bf16[64,64,128]{2,1,0:T(8,128)(2,1)S(1)}, u32[]{:S(2)}, u32[]{:S(2)}) async-start(bf16[64,64,128]{2,1,0:T(8,128)(2,1)} %bitcast.44), calls=%async_computation.3 | async-start | bytes 2097152 | tf_op jit(solution)/shard_map/all_to_all | solution.py:158
  102.8 0.6 reshape.56
  103.4 28.0 %all-to-all-done.3.x_ref = bf16[64,64,128]{2,1,0:T(8,128)(2,1)S(1)} async-done(((bf16[64,64,128]{2,1,0:T(8,128)(2,1)}), bf16[64,64,128]{2,1,0:T(8,128)(2,1)S(1)}, u32[]{:S(2)}, u32[]{:S(2)}) %all-to-all-start.3) | async-done | bytes 1048608 | tf_op jit(solution)/shard_map/all_to_all | solution.py:158
  131.5 1.0 copy-done.1
  132.5 7.7 %shard_map.104 = bf16[64,64,128]{2,1,0:T(8,128)(2,1)} custom-call(bf16[64,64,128]{2,1,0:T(8,128)(2,1)} %copy-done.1, f32[1,4096]{1,0:T(1,128)} %bitcast.52, bf16[3,4096,128]{2,1,0:T(8,128)(2,1)} %pad_maximum_fusion.refs_0_, bf16[3,4096,128]{2,1,0:T(8,128)(2,1)} %collective-permute-done.1.refs_1_, bf16[3,4096,128]{2,1,0:T(8,128)(2,1)} %collective-permute-done.refs_2_, ...), custom_call_target="tpu_custom_call" | custom-call | flops 1610612736 | bytes 14680064 | tf_op jit(solution)/shard_map/pallas_call | solution.py:77
  140.2 5.9 %all-to-all-start.4 = ((bf16[64,64,128]{2,1,0:T(8,128)(2,1)}), bf16[64,64,128]{2,1,0:T(8,128)(2,1)S(1)}, u32[]{:S(2)}, u32[]{:S(2)}) async-start(bf16[64,64,128]{2,1,0:T(8,128)(2,1)} %shard_map.104), calls=%async_computation.4 | async-start | bytes 2097152 | tf_op jit(solution)/shard_map/all_to_all | solution.py:160
  146.2 28.6 %all-to-all-done.4 = bf16[64,64,128]{2,1,0:T(8,128)(2,1)S(1)} async-done(((bf16[64,64,128]{2,1,0:T(8,128)(2,1)}), bf16[64,64,128]{2,1,0:T(8,128)(2,1)S(1)}, u32[]{:S(2)}, u32[]{:S(2)}) %all-to-all-start.4) | async-done | bytes 1048608 | tf_op jit(solution)/shard_map/all_to_all | solution.py:160
  175.0 0.7 reshape.54
  175.6 4.6 %all-to-all-start.5 = ((bf16[12,20,128]{2,1,0:T(8,128)(2,1)}), bf16[12,20,128]{2,1,0:T(8,128)(2,1)S(1)}, u32[]{:S(2)}, u32[]{:S(2)}) async-start(bf16[12,20,128]{2,1,0:T(8,128)(2,1)} %reshape.54), calls=%async_computation.5 | async-start | bytes 147456 | tf_op jit(solution)/shard_map/all_to_all | solution.py:164
  180.3 0.8 slice_bitcast_fusion
  181.1 8.9 %all-to-all-done.5 = bf16[12,20,128]{2,1,0:T(8,128)(2,1)S(1)} async-done(((bf16[12,20,128]{2,1,0:T(8,128)(2,1)}), bf16[12,20,128]{2,1,0:T(8,128)(2,1)S(1)}, u32[]{:S(2)}, u32[]{:S(2)}) %all-to-all-start.5) | async-done | bytes 61472 | tf_op jit(solution)/shard_map/all_to_all | solution.py:164
  190.5 0.9 add_convert_fusion
  (45 shorter events, 2.3 us)
Async XLA Ops:
  0.6 60.5 %copy-start = (bf16[192,4096]{1,0:T(8,128)(2,1)S(1)}, bf16[192,4096]{1,0:T(8,128)(2,1)}, u32[]{:S(2)}) copy-start(bf16[192,4096]{1,0:T(8,128)(2,1)} %param.10) | copy-start | bytes 4718596
  2.3 18.0 %copy-start.2 = (bf16[1,128,4096]{2,1,0:T(8,128)(2,1)S(1)}, bf16[1,128,4096]{2,1,0:T(8,128)(2,1)}, u32[]{:S(2)}) copy-start(bf16[1,128,4096]{2,1,0:T(8,128)(2,1)} %param.17) | copy-start | bytes 3145732
  3.2 36.9 %all-to-all-start = ((bf16[12,64,384]{2,1,0:T(8,128)(2,1)}), bf16[12,64,384]{2,1,0:T(8,128)(2,1)S(1)}, u32[]{:S(2)}, u32[]{:S(2)}) async-start(bf16[12,64,384]{2,1,0:T(8,128)(2,1)} %copy.34), calls=%async_computation | async-start | bytes 1179648 | tf_op jit(solution)/shard_map/all_to_all | solution.py:135
  20.2 1.2 copy-start.3
  20.2 1.5 copy-start.4
  21.7 25.9 %copy-start.7 = (s32[192,2]{0,1:T(2,128)S(1)}, s32[192,2]{0,1:T(2,128)}, u32[]{:S(2)}) copy-start(s32[192,2]{0,1:T(2,128)} %param.13) | copy-start | bytes 4612
  23.7 37.4 %copy-start.5 = (bf16[192,64]{0,1:T(8,128)(2,1)S(1)}, bf16[192,64]{0,1:T(8,128)(2,1)}, u32[]{:S(2)}) copy-start(bf16[192,64]{0,1:T(8,128)(2,1)} %param.9) | copy-start | bytes 73732
  23.7 40.4 %collective-permute-start = (bf16[3,4096,128]{2,1,0:T(8,128)(2,1)}, bf16[3,4096,128]{2,1,0:T(8,128)(2,1)}, u32[]{:S(2)}, u32[]{:S(2)}) collective-permute-start(bf16[3,4096,128]{2,1,0:T(8,128)(2,1)} %pad_maximum_fusion.refs_0_), channel_id=1, source_target_pairs={{0,2},{1,15},{2,0},{3,5},{4,6},{5,3},{6,4},{7,9},{8,10},{9,7},{10,... | collective-permute-start | bytes 9437192 | tf_op jit(solution)/shard_map/ppermute | solution.py:129
  41.1 19.9 %all-to-all-start.1 = ((bf16[12,64,384]{2,1,0:T(8,128)(2,1)}), bf16[12,64,384]{2,1,0:T(8,128)(2,1)S(1)}, u32[]{:S(2)}, u32[]{:S(2)}) async-start(bf16[12,64,384]{2,1,0:T(8,128)(2,1)} %broadcast_in_dim.7), calls=%async_computation.1 | async-start | bytes 1179648 | tf_op jit(solution)/shard_map/all_to_all | solution.py:138
  61.1 41.7 %copy-start.6 = (bf16[4096]{0:T(1024)(128)(2,1)S(1)}, bf16[4096]{0:T(1024)(128)(2,1)}, u32[]{:S(2)}) copy-start(bf16[4096]{0:T(1024)(128)(2,1)} %param.12) | copy-start | bytes 24580
  65.3 18.9 %all-to-all-start.2 = ((bf16[12,20,128]{2,1,0:T(8,128)(2,1)}), bf16[12,20,128]{2,1,0:T(8,128)(2,1)S(1)}, u32[]{:S(2)}, u32[]{:S(2)}) async-start(bf16[12,20,128]{2,1,0:T(8,128)(2,1)} %pad_maximum_fusion.2), calls=%async_computation.2 | async-start | bytes 147456 | tf_op jit(solution)/shard_map/all_to_all | solution.py:154
  74.4 29.1 %collective-permute-start.1 = (bf16[3,4096,128]{2,1,0:T(8,128)(2,1)}, bf16[3,4096,128]{2,1,0:T(8,128)(2,1)}, u32[]{:S(2)}, u32[]{:S(2)}) collective-permute-start(bf16[3,4096,128]{2,1,0:T(8,128)(2,1)} %pad_maximum_fusion.refs_0_), channel_id=1, source_target_pairs={{0,1},{1,0},{2,3},{3,2},{4,5},{5,4},{6,7},{7,6},{8,9},{9,8},{10,11... | collective-permute-start | bytes 9437192 | tf_op jit(solution)/shard_map/ppermute | solution.py:130
  82.3 21.2 %collective-permute-start.2 = (bf16[3,4096,128]{2,1,0:T(8,128)(2,1)}, bf16[3,4096,128]{2,1,0:T(8,128)(2,1)}, u32[]{:S(2)}, u32[]{:S(2)}) collective-permute-start(bf16[3,4096,128]{2,1,0:T(8,128)(2,1)} %collective-permute-done.refs_2_), channel_id=1, source_target_pairs={{0,1},{1,0},{2,3},{3,2},{4,5},{5,4},{6,7},{7,6},{8,9},{9,8},{10,11... | collective-permute-start | bytes 9437192 | tf_op jit(solution)/shard_map/ppermute | solution.py:146
  85.6 45.9 %all-to-all-start.3 = ((bf16[64,64,128]{2,1,0:T(8,128)(2,1)}), bf16[64,64,128]{2,1,0:T(8,128)(2,1)S(1)}, u32[]{:S(2)}, u32[]{:S(2)}) async-start(bf16[64,64,128]{2,1,0:T(8,128)(2,1)} %bitcast.44), calls=%async_computation.3 | async-start | bytes 2097152 | tf_op jit(solution)/shard_map/all_to_all | solution.py:158
  131.5 1.0 copy-start.1
  132.5 13.7 %copy-start.8 = (s32[192,2]{0,1:T(2,128)S(1)}, s32[192,2]{0,1:T(2,128)}, u32[]{:S(2)}) copy-start(s32[192,2]{0,1:T(2,128)} %param.14) | copy-start | bytes 4612
  140.2 34.6 %all-to-all-start.4 = ((bf16[64,64,128]{2,1,0:T(8,128)(2,1)}), bf16[64,64,128]{2,1,0:T(8,128)(2,1)S(1)}, u32[]{:S(2)}, u32[]{:S(2)}) async-start(bf16[64,64,128]{2,1,0:T(8,128)(2,1)} %shard_map.104), calls=%async_computation.4 | async-start | bytes 2097152 | tf_op jit(solution)/shard_map/all_to_all | solution.py:160
  175.6 14.3 %all-to-all-start.5 = ((bf16[12,20,128]{2,1,0:T(8,128)(2,1)}), bf16[12,20,128]{2,1,0:T(8,128)(2,1)S(1)}, u32[]{:S(2)}, u32[]{:S(2)}) async-start(bf16[12,20,128]{2,1,0:T(8,128)(2,1)} %reshape.54), calls=%async_computation.5 | async-start | bytes 147456 | tf_op jit(solution)/shard_map/all_to_all | solution.py:164

commit v2 on v1

--- a/solution.py
+++ b/solution.py
@@ -1,3 +1,5 @@
+import functools
+
 import jax
 import jax.numpy as jnp
 from jax import lax
@@ -7,6 +9,8 @@
 
 epsilon = 1e-05
 MEMBERS = 4
+ROWS = 16
+SLOT_ROWS = 32
 RING = 8
 SHARD = ("group", "chip", "core")
 LANES = 128
@@ -91,6 +95,73 @@
     )(x, gain, *weights)
 
 
+def tile_of(number, width):
+    across = width // LANES
+    row, column = number // across * ROWS, number % across * LANES
+    return slice(row, row + ROWS), slice(column, column + LANES)
+
+
+def cut_kernel(columns_ref, out_ref):
+    feats, width = columns_ref.shape
+    tiles = feats // ROWS * (width // LANES)
+    for t in range(tiles):
+        rows, lanes = tile_of(t, width)
+        out_ref[t * ROWS : (t + 1) * ROWS, :] = columns_ref[rows, lanes]
+    if tiles * ROWS < out_ref.shape[0]:
+        out_ref[tiles * ROWS :, :] = jnp.zeros((out_ref.shape[0] - tiles * ROWS, LANES), BF16)
+
+
+def cut(columns, out_rows):
+    return pl.pallas_call(
+        cut_kernel,
+        out_shape=jax.ShapeDtypeStruct((out_rows, LANES), BF16),
+        in_specs=[pl.BlockSpec(memory_space=pltpu.VMEM)],
+        out_specs=pl.BlockSpec(memory_space=pltpu.VMEM),
+        cost_estimate=pl.CostEstimate(flops=0, bytes_accessed=4 * columns.size, transcendentals=0),
+    )(columns)
+
+
+def hidden_kernel(half_cap, parts_ref, context_ref, resid_ref, slots_ref, merged_ref, hidden_ref, sent_ref):
+    feats, width = merged_ref.shape
+    tokens = context_ref.shape[0]
+    for t in range(feats // ROWS * (width // LANES)):
+        rows, lanes = tile_of(t, width)
+        merged_ref[rows, lanes] = parts_ref[t * ROWS : (t + 1) * ROWS, :]
+    across = (((1,), (1,)), ((), ()))
+    product = lax.dot_general(merged_ref[...], context_ref[...], across, preferred_element_type=F32)
+    hidden = (resid_ref[...].astype(F32) + product).astype(BF16)
+    hidden_ref[...] = hidden
+    count = sent_ref.shape[0]
+    row = lax.broadcasted_iota(jnp.int32, (count, tokens), 0)
+    place, expert = row % SLOT_ROWS, row // SLOT_ROWS
+    empty = jnp.zeros((LANES - feats, tokens), BF16)
+    sent = jnp.zeros((count, LANES), F32)
+    for side in range(2):
+        slot = jnp.where(place < half_cap, (2 * expert + side) * half_cap + place, -1)
+        table = ((slots_ref[0:1, :] == slot) | (slots_ref[1:2, :] == slot)).astype(F32).astype(BF16)
+        lanes = jnp.concatenate([hidden, empty] if side == 0 else [empty, hidden], axis=0)
+        sent += lax.dot_general(table, lanes, across, preferred_element_type=F32)
+    sent_ref[...] = sent.astype(BF16)
+
+
+def hidden_rows(parts, context, resid, slots, n_experts, half_cap):
+    feats, tokens = resid.shape
+    width = context.shape[1]
+    return pl.pallas_call(
+        functools.partial(hidden_kernel, half_cap),
+        out_shape=(
+            jax.ShapeDtypeStruct((feats, width), BF16),
+            jax.ShapeDtypeStruct((feats, tokens), BF16),
+            jax.ShapeDtypeStruct((n_experts * SLOT_ROWS, LANES), BF16),
+        ),
+        in_specs=[pl.BlockSpec(memory_space=pltpu.VMEM)] * 4,
+        out_specs=[pl.BlockSpec(memory_space=pltpu.VMEM)] * 3,
+        cost_estimate=pl.CostEstimate(
+            flops=2 * feats * tokens * width, bytes_accessed=2 * (2 * feats + tokens) * width, transcendentals=0
+        ),
+    )(parts, context, resid, slots)
+
+
 def ring_pairs(shards):
     pairs = []
     for source in range(shards):
@@ -129,29 +200,20 @@
     beside = lax.ppermute(own, SHARD, ring_pairs(shards))
     own_core = lax.ppermute(own, "core", [(0, 1), (1, 0)])
 
-    piece = -(-full_width // (LANES * n_experts)) * LANES
-    missing = n_experts * piece - full_width
-    columns = jnp.pad(o_weight[0].T, ((0, 0), (0, missing))).reshape(feat_width, n_experts, piece)
-    parts = lax.all_to_all(columns.transpose(1, 0, 2), "branch", 0, 0, tiled=True)
+    piece = -(-(full_width * feat_width) // (LANES * ROWS * n_experts)) * ROWS
+    tiles = cut(o_weight[0].T, n_experts * piece).reshape(n_experts, piece, LANES)
+    parts = lax.all_to_all(tiles, "branch", 0, 0, tiled=True)
     mean_part = (jnp.sum(parts.astype(F32), axis=0) / n_experts).astype(BF16)
-    spread = jnp.broadcast_to(mean_part[None], (n_experts, feat_width, piece))
-    merged = lax.all_to_all(spread, "branch", 0, 0, tiled=True)
-    merged = merged.transpose(1, 0, 2).reshape(feat_width, n_experts * piece)[:, :full_width].T
-
-    hidden_state = (
-        resid.astype(F32) + jnp.dot(context, merged, preferred_element_type=F32)
-    ).astype(BF16)
-
+    spread = jnp.broadcast_to(mean_part[None], (n_experts, piece, LANES))
+    all_parts = lax.all_to_all(spread, "branch", 0, 0, tiled=True).reshape(n_experts * piece, LANES)
+
+    slots = slot_index(expert_ids, n_experts, capacity)
+    merged, hidden, sent = hidden_rows(all_parts, context, resid.T, slots.T, n_experts, half_cap)
+    merged, hidden_state = merged.T, hidden.T
     hidden_state, beside = lax.optimization_barrier((hidden_state, beside))
     beside_core = lax.ppermute(beside, "core", [(0, 1), (1, 0)])
-
-    slots = slot_index(expert_ids, n_experts, capacity)
-    all_slots = jnp.arange(n_experts * capacity, dtype=jnp.int32)
-    pick_table = ((slots[None, :, 0] == all_slots[:, None]) | (slots[None, :, 1] == all_slots[:, None])).astype(BF16)
-    sent = jnp.dot(pick_table, hidden_state, preferred_element_type=F32).astype(BF16)
-    sent = sent.reshape(n_experts, 2, half_cap, feat_width)
-    sent = jnp.concatenate([sent[:, 0], sent[:, 1]], axis=2)
-    arrived = lax.all_to_all(sent, "branch", 0, 0, tiled=True)
+    arrived = lax.all_to_all(sent.reshape(n_experts, SLOT_ROWS, LANES), "branch", 0, 0, tiled=True)
+    arrived = arrived[:, :half_cap]
 
     quarters = jnp.pad(arrived.reshape(MEMBERS, quarter, LANES), ((0, 0), (0, half - quarter), (0, 0)))
     copies = jnp.broadcast_to(quarters[None], (n_groups, MEMBERS, half, LANES)).reshape(shards, half, LANES)
@@ -164,6 +226,7 @@
     returned = lax.all_to_all(expert_out, "branch", 0, 0, tiled=True)
     returned = jnp.stack([returned[:, :, :feat_width], returned[:, :, feat_width:]], axis=1)
     returned = returned.reshape(n_experts * capacity, feat_width)
+    all_slots = jnp.arange(n_experts * capacity, dtype=jnp.int32)
     code_vals = combine_codes.astype(F32)
     mix_weights = code_vals / jnp.sum(code_vals, axis=1, keepdims=True)
     mixture = jnp.zeros((tok_rows, feat_width), F32)

time: 192 us -> 190 us (0.990)
  waiting for transfers between devices: 91.6 us -> 86 us
  Pallas kernels: 7.71 us -> 12.9 us
  local copies, waits for them, and re-layouts: 9.72 us -> 5.3 us
  starting transfers between devices: 75.4 us -> 77.9 us
    pallas_call x0 -> x2, Pallas kernels: none -> 5.15 us  [the longest x1 3.22 us: hidden_rows(): pl.pallas_call(functools.partial(hidden_kernel, half_cap), out_shape=(jax...]
    all_to_all x3, waiting for transfers between devices: 23.8 us -> 19.7 us  [the longest x1 11 us: local(): lax.all_to_all(spread, 'branch', 0, 0, tiled=True)]
    all_to_all x1, starting transfers between devices: 17.3 us -> 19.7 us  [local(): gathered = lax.all_to_all(copies, SHARD, 0, 0, tiled=True)]
    ppermute x1, waiting for transfers between devices: 2.36 us -> 0.01 us  [local(): beside = lax.ppermute(own, SHARD, ring_pairs(shards))]
    ppermute x1, starting transfers between devices: 7.92 us -> 10.1 us  [local(): own_core = lax.ppermute(own, 'core', [(0, 1), (1, 0)])]
    all_to_all x3, starting transfers between devices: 32.6 us -> 30.6 us  [the longest x1 17 us: local(): parts = lax.all_to_all(tiles, 'branch', 0, 0, tiled=True)]
  transfers between devices with their start and end apart: 9 -> 9, of which waited for: 6 -> 5; matrix products, arithmetic and copies ran while one was open for 4% -> 5% of each run, Pallas kernels for 0% -> 2%
where the time goes in v2:
time: 190 us; the launch traced here: 189 us
  waiting for transfers between devices  86 us (45%)
  starting transfers between devices  77.9 us (41%)
  Pallas kernels  12.9 us (7%)
  local copies, waits for them, and re-layouts  5.3 us (3%)
  other arithmetic  5.13 us (3%)
    all_to_all x1, waiting for transfers between devices, local(): exchanged = lax.all_to_all(partial_out, SHARD, 0, 0, tiled=True)  28.6 us
    all_to_all x1, waiting for transfers between devices, local(): gathered = lax.all_to_all(copies, SHARD, 0, 0, tiled=True)  28 us
    all_to_all x1, starting transfers between devices, local(): gathered = lax.all_to_all(copies, SHARD, 0, 0, tiled=True)  19.7 us
    all_to_all x1, starting transfers between devices, local(): parts = lax.all_to_all(tiles, 'branch', 0, 0, tiled=True)  17 us
    all_to_all x1, waiting for transfers between devices, local(): lax.all_to_all(spread, 'branch', 0, 0, tiled=True)  11 us
    ppermute x1, starting transfers between devices, local(): own_core = lax.ppermute(own, 'core', [(0, 1), (1, 0)])  10.1 us
    all_to_all x1, waiting for transfers between devices, local(): returned = lax.all_to_all(expert_out, 'branch', 0, 0, tiled=True)  9.71 us
    all_to_all x1, waiting for transfers between devices, local(): parts = lax.all_to_all(tiles, 'branch', 0, 0, tiled=True)  8.73 us
  transfers between devices with their start and end apart: 9, of which 5 were waited for; matrix products, arithmetic and copies ran while one was open for 5% of the time, Pallas kernels for 2%

profile of v2, /device:TPU:1, one launch (start us, length us, event | category | flops | bytes accessed | tf_op | source)
XLA Modules:
  0.0 188.9 jit_solution(13167731859934997734)
XLA Ops:
  0.6 1.9 %shard_map.104 = bf16[2112,128]{1,0:T(8,128)(2,1)} custom-call(bf16[64,4096]{1,0:T(8,128)(2,1)} %bitcast.36), custom_call_target="tpu_custom_call" | custom-call | bytes 1048576 | tf_op jit(solution)/shard_map/pallas_call | solution.py:115
  2.6 17.0 %all-to-all-start = ((bf16[12,176,128]{2,1,0:T(8,128)(2,1)}), bf16[12,176,128]{2,1,0:T(8,128)(2,1)}, u32[]{:S(2)}, u32[]{:S(2)}) async-start(bf16[12,176,128]{2,1,0:T(8,128)(2,1)} %bitcast.34), calls=%async_computation | async-start | bytes 1081344 | tf_op jit(solution)/shard_map/all_to_all | solution.py:205
  19.5 1.4 copy.16
  21.0 0.4 copy.14
  21.4 1.9 pad_maximum_fusion.refs_0_
  23.3 5.1 %collective-permute-start = (bf16[3,4096,128]{2,1,0:T(8,128)(2,1)S(1)}, bf16[3,4096,128]{2,1,0:T(8,128)(2,1)}, u32[]{:S(2)}, u32[]{:S(2)}) collective-permute-start(bf16[3,4096,128]{2,1,0:T(8,128)(2,1)S(1)} %pad_maximum_fusion.refs_0_), channel_id=1, source_target_pairs={{0,2},{1,15},{2,0},{3,5},{4,6},{5,3},{6,4},{7,9},{8,10},{9,7},{10,... | collective-permute-start | bytes 9437192 | tf_op jit(solution)/shard_map/ppermute | solution.py:200
  28.4 8.7 %all-to-all-done = bf16[12,176,128]{2,1,0:T(8,128)(2,1)} async-done(((bf16[12,176,128]{2,1,0:T(8,128)(2,1)}), bf16[12,176,128]{2,1,0:T(8,128)(2,1)}, u32[]{:S(2)}, u32[]{:S(2)}) %all-to-all-start) | async-done | bytes 540704 | tf_op jit(solution)/shard_map/all_to_all | solution.py:205
  37.2 1.1 convert_reduce_fusion
  38.3 0.9 broadcast_in_dim.7
  39.2 8.4 %all-to-all-start.1 = ((bf16[12,176,128]{2,1,0:T(8,128)(2,1)}), bf16[12,176,128]{2,1,0:T(8,128)(2,1)}, u32[]{:S(2)}, u32[]{:S(2)}) async-start(bf16[12,176,128]{2,1,0:T(8,128)(2,1)} %broadcast_in_dim.7), calls=%async_computation.1 | async-start | bytes 1081344 | tf_op jit(solution)/shard_map/all_to_all | solution.py:208
  47.8 0.1 eq.45
  47.9 0.2 fusion.1
  48.3 0.6 multiply_add_fusion
  49.0 11.0 %all-to-all-done.1 = bf16[12,176,128]{2,1,0:T(8,128)(2,1)} async-done(((bf16[12,176,128]{2,1,0:T(8,128)(2,1)}), bf16[12,176,128]{2,1,0:T(8,128)(2,1)}, u32[]{:S(2)}, u32[]{:S(2)}) %all-to-all-start.1) | async-done | bytes 540704 | tf_op jit(solution)/shard_map/all_to_all | solution.py:208
  59.9 3.2 %shard_map.105 = (bf16[64,4096]{1,0:T(8,128)(2,1)}, bf16[64,192]{1,0:T(8,128)(2,1)}, bf16[384,128]{1,0:T(8,128)(2,1)}) custom-call(bf16[2112,128]{1,0:T(8,128)(2,1)} %bitcast.3.parts_ref, bf16[192,4096]{1,0:T(8,128)(2,1)} %context_ref.1, bf16[64,192]{1,0:T(8,128)(2,1)} %bitcast.40, s32[2,192]{1,0:T(2,128)} %bitcast.42), custom_call_target="tpu_custom_call" | custom-call | flops 100663296 | bytes 2621440 | tf_op jit(solution)/shard_map/pallas_call | solution.py:150
  63.2 5.2 %all-to-all-start.2 = ((bf16[12,32,128]{2,1,0:T(8,128)(2,1)}), bf16[12,32,128]{2,1,0:T(8,128)(2,1)S(1)}, u32[]{:S(2)}, u32[]{:S(2)}) async-start(bf16[12,32,128]{2,1,0:T(8,128)(2,1)} %bitcast.38), calls=%async_computation.2 | async-start | bytes 196608 | tf_op jit(solution)/shard_map/all_to_all | solution.py:215
  68.4 10.1 %collective-permute-start.1 = (bf16[3,4096,128]{2,1,0:T(8,128)(2,1)S(1)}, bf16[3,4096,128]{2,1,0:T(8,128)(2,1)}, u32[]{:S(2)}, u32[]{:S(2)}) collective-permute-start(bf16[3,4096,128]{2,1,0:T(8,128)(2,1)S(1)} %pad_maximum_fusion.refs_0_), channel_id=1, source_target_pairs={{0,1},{1,0},{2,3},{3,2},{4,5},{5,4},{6,7},{7,6},{8,9},{9,8},{10,11... | collective-permute-start | bytes 9437192 | tf_op jit(solution)/shard_map/ppermute | solution.py:201
  78.5 1.9 %collective-permute-start.2 = (bf16[3,4096,128]{2,1,0:T(8,128)(2,1)}, bf16[3,4096,128]{2,1,0:T(8,128)(2,1)}, u32[]{:S(2)}, u32[]{:S(2)}) collective-permute-start(bf16[3,4096,128]{2,1,0:T(8,128)(2,1)} %collective-permute-done.refs_2_), channel_id=1, source_target_pairs={{0,1},{1,0},{2,3},{3,2},{4,5},{5,4},{6,7},{7,6},{8,9},{9,8},{10,11... | collective-permute-start | bytes 9437192 | tf_op jit(solution)/shard_map/ppermute | solution.py:214
  80.5 1.2 broadcast_in_dim.10
  81.8 19.7 %all-to-all-start.3 = ((bf16[64,64,128]{2,1,0:T(8,128)(2,1)}), bf16[64,64,128]{2,1,0:T(8,128)(2,1)}, u32[]{:S(2)}, u32[]{:S(2)}) async-start(bf16[64,64,128]{2,1,0:T(8,128)(2,1)} %bitcast.31), calls=%async_computation.3 | async-start | bytes 2097152 | tf_op jit(solution)/shard_map/all_to_all | solution.py:220
  101.5 0.6 reshape.54
  102.1 28.0 %all-to-all-done.3.x_ref = bf16[64,64,128]{2,1,0:T(8,128)(2,1)} async-done(((bf16[64,64,128]{2,1,0:T(8,128)(2,1)}), bf16[64,64,128]{2,1,0:T(8,128)(2,1)}, u32[]{:S(2)}, u32[]{:S(2)}) %all-to-all-start.3) | async-done | bytes 1048608 | tf_op jit(solution)/shard_map/all_to_all | solution.py:220
  130.1 7.7 %shard_map.106 = bf16[64,64,128]{2,1,0:T(8,128)(2,1)} custom-call(bf16[64,64,128]{2,1,0:T(8,128)(2,1)} %all-to-all-done.3.x_ref, f32[1,4096]{1,0:T(1,128)} %bitcast.39, bf16[3,4096,128]{2,1,0:T(8,128)(2,1)} %copy-done, bf16[3,4096,128]{2,1,0:T(8,128)(2,1)} %collective-permute-done.1.refs_1_, bf16[3,4096,128]{2,1,0:T(8,128)(2,1)} %collective-permute-done.refs_2_, ...), custom_call_target="tpu_custom_call" | custom-call | flops 1610612736 | bytes 14680064 | tf_op jit(solution)/shard_map/pallas_call | solution.py:81
  137.8 5.9 %all-to-all-start.4 = ((bf16[64,64,128]{2,1,0:T(8,128)(2,1)}), bf16[64,64,128]{2,1,0:T(8,128)(2,1)S(1)}, u32[]{:S(2)}, u32[]{:S(2)}) async-start(bf16[64,64,128]{2,1,0:T(8,128)(2,1)} %shard_map.106), calls=%async_computation.4 | async-start | bytes 2097152 | tf_op jit(solution)/shard_map/all_to_all | solution.py:222
  143.8 28.6 %all-to-all-done.4 = bf16[64,64,128]{2,1,0:T(8,128)(2,1)S(1)} async-done(((bf16[64,64,128]{2,1,0:T(8,128)(2,1)}), bf16[64,64,128]{2,1,0:T(8,128)(2,1)S(1)}, u32[]{:S(2)}, u32[]{:S(2)}) %all-to-all-start.4) | async-done | bytes 1048608 | tf_op jit(solution)/shard_map/all_to_all | solution.py:222
  172.3 0.2 reduce_sum.41
  172.5 0.6 reshape.52
  173.2 4.6 %all-to-all-start.5 = ((bf16[12,20,128]{2,1,0:T(8,128)(2,1)}), bf16[12,20,128]{2,1,0:T(8,128)(2,1)S(1)}, u32[]{:S(2)}, u32[]{:S(2)}) async-start(bf16[12,20,128]{2,1,0:T(8,128)(2,1)} %reshape.52), calls=%async_computation.5 | async-start | bytes 147456 | tf_op jit(solution)/shard_map/all_to_all | solution.py:226
  177.8 9.7 %all-to-all-done.5 = bf16[12,20,128]{2,1,0:T(8,128)(2,1)S(1)} async-done(((bf16[12,20,128]{2,1,0:T(8,128)(2,1)}), bf16[12,20,128]{2,1,0:T(8,128)(2,1)S(1)}, u32[]{:S(2)}, u32[]{:S(2)}) %all-to-all-start.5) | async-done | bytes 61472 | tf_op jit(solution)/shard_map/all_to_all | solution.py:226
  187.7 0.3 convolution_multiply_fusion.1
  188.0 0.3 fusion
  188.3 0.6 add_convert_fusion
  (32 shorter events, 0.7 us)
Async XLA Ops:
  2.6 34.6 %all-to-all-start = ((bf16[12,176,128]{2,1,0:T(8,128)(2,1)}), bf16[12,176,128]{2,1,0:T(8,128)(2,1)}, u32[]{:S(2)}, u32[]{:S(2)}) async-start(bf16[12,176,128]{2,1,0:T(8,128)(2,1)} %bitcast.34), calls=%async_computation | async-start | bytes 1081344 | tf_op jit(solution)/shard_map/all_to_all | solution.py:205
  21.4 26.2 %copy-start.4 = (s32[192,2]{0,1:T(2,128)S(1)}, s32[192,2]{0,1:T(2,128)}, u32[]{:S(2)}) copy-start(s32[192,2]{0,1:T(2,128)} %param.13) | copy-start | bytes 4612
  23.3 58.4 %copy-start = (bf16[3,4096,128]{2,1,0:T(8,128)(2,1)}, bf16[3,4096,128]{2,1,0:T(8,128)(2,1)S(1)}, u32[]{:S(2)}) copy-start(bf16[3,4096,128]{2,1,0:T(8,128)(2,1)S(1)} %pad_maximum_fusion.refs_0_) | copy-start | bytes 9437188
  23.3 55.2 %collective-permute-start = (bf16[3,4096,128]{2,1,0:T(8,128)(2,1)S(1)}, bf16[3,4096,128]{2,1,0:T(8,128)(2,1)}, u32[]{:S(2)}, u32[]{:S(2)}) collective-permute-start(bf16[3,4096,128]{2,1,0:T(8,128)(2,1)S(1)} %pad_maximum_fusion.refs_0_), channel_id=1, source_target_pairs={{0,2},{1,15},{2,0},{3,5},{4,6},{5,3},{6,4},{7,9},{8,10},{9,7},{10,... | collective-permute-start | bytes 9437192 | tf_op jit(solution)/shard_map/ppermute | solution.py:200
  39.2 20.8 %all-to-all-start.1 = ((bf16[12,176,128]{2,1,0:T(8,128)(2,1)}), bf16[12,176,128]{2,1,0:T(8,128)(2,1)}, u32[]{:S(2)}, u32[]{:S(2)}) async-start(bf16[12,176,128]{2,1,0:T(8,128)(2,1)} %broadcast_in_dim.7), calls=%async_computation.1 | async-start | bytes 1081344 | tf_op jit(solution)/shard_map/all_to_all | solution.py:208
  47.9 53.6 %copy-start.3 = (bf16[4096]{0:T(1024)(128)(2,1)S(1)}, bf16[4096]{0:T(1024)(128)(2,1)}, u32[]{:S(2)}) copy-start(bf16[4096]{0:T(1024)(128)(2,1)} %param.12) | copy-start | bytes 24580
  63.2 17.3 %all-to-all-start.2 = ((bf16[12,32,128]{2,1,0:T(8,128)(2,1)}), bf16[12,32,128]{2,1,0:T(8,128)(2,1)S(1)}, u32[]{:S(2)}, u32[]{:S(2)}) async-start(bf16[12,32,128]{2,1,0:T(8,128)(2,1)} %bitcast.38), calls=%async_computation.2 | async-start | bytes 196608 | tf_op jit(solution)/shard_map/all_to_all | solution.py:215
  68.4 33.7 %collective-permute-start.1 = (bf16[3,4096,128]{2,1,0:T(8,128)(2,1)S(1)}, bf16[3,4096,128]{2,1,0:T(8,128)(2,1)}, u32[]{:S(2)}, u32[]{:S(2)}) collective-permute-start(bf16[3,4096,128]{2,1,0:T(8,128)(2,1)S(1)} %pad_maximum_fusion.refs_0_), channel_id=1, source_target_pairs={{0,1},{1,0},{2,3},{3,2},{4,5},{5,4},{6,7},{7,6},{8,9},{9,8},{10,11... | collective-permute-start | bytes 9437192 | tf_op jit(solution)/shard_map/ppermute | solution.py:201
  78.5 23.6 %collective-permute-start.2 = (bf16[3,4096,128]{2,1,0:T(8,128)(2,1)}, bf16[3,4096,128]{2,1,0:T(8,128)(2,1)}, u32[]{:S(2)}, u32[]{:S(2)}) collective-permute-start(bf16[3,4096,128]{2,1,0:T(8,128)(2,1)} %collective-permute-done.refs_2_), channel_id=1, source_target_pairs={{0,1},{1,0},{2,3},{3,2},{4,5},{5,4},{6,7},{7,6},{8,9},{9,8},{10,11... | collective-permute-start | bytes 9437192 | tf_op jit(solution)/shard_map/ppermute | solution.py:214
  81.8 48.3 %all-to-all-start.3 = ((bf16[64,64,128]{2,1,0:T(8,128)(2,1)}), bf16[64,64,128]{2,1,0:T(8,128)(2,1)}, u32[]{:S(2)}, u32[]{:S(2)}) async-start(bf16[64,64,128]{2,1,0:T(8,128)(2,1)} %bitcast.31), calls=%async_computation.3 | async-start | bytes 2097152 | tf_op jit(solution)/shard_map/all_to_all | solution.py:220
  130.1 13.6 %copy-start.5 = (s32[192,2]{0,1:T(2,128)S(1)}, s32[192,2]{0,1:T(2,128)}, u32[]{:S(2)}) copy-start(s32[192,2]{0,1:T(2,128)} %param.14) | copy-start | bytes 4612
  130.1 13.7 %copy-start.2 = (s32[192,2]{0,1:T(2,128)S(1)}, s32[192,2]{0,1:T(2,128)}, u32[]{:S(2)}) copy-start(s32[192,2]{0,1:T(2,128)} %multiply_add_fusion) | copy-start | bytes 4612
  137.8 50.5 %copy-start.1 = (bf16[64,192]{1,0:T(8,128)(2,1)S(1)}, bf16[64,192]{1,0:T(8,128)(2,1)}, u32[]{:S(2)}) copy-start(bf16[64,192]{1,0:T(8,128)(2,1)} %get-tuple-element.7) | copy-start | bytes 73732
  137.8 34.5 %all-to-all-start.4 = ((bf16[64,64,128]{2,1,0:T(8,128)(2,1)}), bf16[64,64,128]{2,1,0:T(8,128)(2,1)S(1)}, u32[]{:S(2)}, u32[]{:S(2)}) async-start(bf16[64,64,128]{2,1,0:T(8,128)(2,1)} %shard_map.106), calls=%async_computation.4 | async-start | bytes 2097152 | tf_op jit(solution)/shard_map/all_to_all | solution.py:222
  173.2 14.4 %all-to-all-start.5 = ((bf16[12,20,128]{2,1,0:T(8,128)(2,1)}), bf16[12,20,128]{2,1,0:T(8,128)(2,1)S(1)}, u32[]{:S(2)}, u32[]{:S(2)}) async-start(bf16[12,20,128]{2,1,0:T(8,128)(2,1)} %reshape.52), calls=%async_computation.5 | async-start | bytes 147456 | tf_op jit(solution)/shard_map/all_to_all | solution.py:226

commit v3 on v2

--- a/solution.py
+++ b/solution.py
@@ -162,6 +162,36 @@
     )(parts, context, resid, slots)
 
 
+def combine_kernel(half_cap, returned_ref, hidden_ref, slots_ref, weights_ref, mixed_ref):
+    feats, tokens = hidden_ref.shape
+    count = returned_ref.shape[0]
+    row = lax.broadcasted_iota(jnp.int32, (count, tokens), 0)
+    place, expert = row % SLOT_ROWS, row // SLOT_ROWS
+    down = (((0,), (0,)), ((), ()))
+    mixed = hidden_ref[...].astype(F32)
+    for k in range(2):
+        picked = jnp.zeros((feats, tokens), F32)
+        for side in range(2):
+            slot = jnp.where(place < half_cap, (2 * expert + side) * half_cap + place, -1)
+            table = (slots_ref[k : k + 1, :] == slot).astype(F32).astype(BF16)
+            both = lax.dot_general(returned_ref[...], table, down, preferred_element_type=F32)
+            picked += both[side * feats : (side + 1) * feats, :]
+        mixed += picked * weights_ref[k : k + 1, :]
+    mixed_ref[...] = mixed.astype(BF16)
+
+
+def combine(returned, hidden, slots, weights, half_cap):
+    return pl.pallas_call(
+        functools.partial(combine_kernel, half_cap),
+        out_shape=jax.ShapeDtypeStruct(hidden.shape, BF16),
+        in_specs=[pl.BlockSpec(memory_space=pltpu.VMEM)] * 4,
+        out_specs=pl.BlockSpec(memory_space=pltpu.VMEM),
+        cost_estimate=pl.CostEstimate(
+            flops=8 * returned.size * hidden.shape[1], bytes_accessed=2 * returned.size, transcendentals=0
+        ),
+    )(returned, hidden, slots, weights)
+
+
 def ring_pairs(shards):
     pairs = []
     for source in range(shards):
@@ -209,8 +239,7 @@
 
     slots = slot_index(expert_ids, n_experts, capacity)
     merged, hidden, sent = hidden_rows(all_parts, context, resid.T, slots.T, n_experts, half_cap)
-    merged, hidden_state = merged.T, hidden.T
-    hidden_state, beside = lax.optimization_barrier((hidden_state, beside))
+    hidden, beside = lax.optimization_barrier((hidden, beside))
     beside_core = lax.ppermute(beside, "core", [(0, 1), (1, 0)])
     arrived = lax.all_to_all(sent.reshape(n_experts, SLOT_ROWS, LANES), "branch", 0, 0, tiled=True)
     arrived = arrived[:, :half_cap]
@@ -223,19 +252,12 @@
     expert_out = jnp.sum(exchanged.reshape(n_groups, MEMBERS, half, LANES).astype(F32), axis=0).astype(BF16)
 
     expert_out = expert_out[:, :quarter].reshape(n_experts, half_cap, LANES)
-    returned = lax.all_to_all(expert_out, "branch", 0, 0, tiled=True)
-    returned = jnp.stack([returned[:, :, :feat_width], returned[:, :, feat_width:]], axis=1)
-    returned = returned.reshape(n_experts * capacity, feat_width)
-    all_slots = jnp.arange(n_experts * capacity, dtype=jnp.int32)
+    expert_out = jnp.pad(expert_out, ((0, 0), (0, SLOT_ROWS - half_cap), (0, 0)))
+    returned = lax.all_to_all(expert_out, "branch", 0, 0, tiled=True).reshape(n_experts * SLOT_ROWS, LANES)
     code_vals = combine_codes.astype(F32)
     mix_weights = code_vals / jnp.sum(code_vals, axis=1, keepdims=True)
-    mixture = jnp.zeros((tok_rows, feat_width), F32)
-    for k in range(2):
-        table = (slots[:, k, None] == all_slots[None, :]).astype(BF16)
-        picked = jnp.dot(table, returned, preferred_element_type=F32)
-        mixture += picked * mix_weights[:, k, None]
-    mixed = (hidden_state.astype(F32) + mixture).astype(BF16)
-    return (mixed, merged)
+    mixed = combine(returned, hidden, slots.T, mix_weights.T, half_cap)
+    return (mixed.T, merged.T)
 
 
 def solution(mesh):

time: 190 us -> 192 us (1.011)
  blocking collectives: 0 us -> 34.5 us
  waiting for transfers between devices: 86 us -> 57.4 us
  starting transfers between devices: 77.9 us -> 72.1 us
    all_to_all x0 -> x1, blocking collectives: none -> 34.5 us  [local(): exchanged = lax.all_to_all(partial_out, SHARD, 0, 0, tiled=True)]
    all_to_all x2 -> x1, waiting for transfers between devices: 38.3 us -> 9.72 us  [local(): lax.all_to_all(expert_out, 'branch', 0, 0, tiled=True)]
    all_to_all x2 -> x1, starting transfers between devices: 10.5 us -> 4.63 us  [local(): lax.all_to_all(expert_out, 'branch', 0, 0, tiled=True)]
  transfers between devices with their start and end apart: 9 -> 8, of which waited for: 5 -> 4; matrix products, arithmetic and copies ran while one was open for 5% -> 5% of each run, Pallas kernels for 2% -> 2%
where the time goes in v3:
time: 192 us; the launch traced here: 191 us
  starting transfers between devices  72.1 us (38%)
  waiting for transfers between devices  57.4 us (30%)
  blocking collectives  34.5 us (18%)
  Pallas kernels  14.7 us (8%)
  local copies, waits for them, and re-layouts  5.8 us (3%)
  other arithmetic  5.04 us (3%)
    all_to_all x1, blocking collectives, local(): exchanged = lax.all_to_all(partial_out, SHARD, 0, 0, tiled=True)  34.5 us
    all_to_all x1, waiting for transfers between devices, local(): gathered = lax.all_to_all(copies, SHARD, 0, 0, tiled=True)  28 us
    all_to_all x1, starting transfers between devices, local(): gathered = lax.all_to_all(copies, SHARD, 0, 0, tiled=True)  19.7 us
    all_to_all x1, starting transfers between devices, local(): parts = lax.all_to_all(tiles, 'branch', 0, 0, tiled=True)  17 us
    all_to_all x1, waiting for transfers between devices, local(): lax.all_to_all(spread, 'branch', 0, 0, tiled=True)  11 us
    ppermute x1, starting transfers between devices, local(): own_core = lax.ppermute(own, 'core', [(0, 1), (1, 0)])  10.1 us
    all_to_all x1, waiting for transfers between devices, local(): lax.all_to_all(expert_out, 'branch', 0, 0, tiled=True)  9.72 us
    all_to_all x1, waiting for transfers between devices, local(): parts = lax.all_to_all(tiles, 'branch', 0, 0, tiled=True)  8.73 us
  transfers between devices with their start and end apart: 8, of which 4 were waited for; matrix products, arithmetic and copies ran while one was open for 5% of the time, Pallas kernels for 2%

profile of v3, /device:TPU:1, one launch (start us, length us, event | category | flops | bytes accessed | tf_op | source)
XLA Modules:
  0.0 190.7 jit_solution(16591506946988934630)
XLA Ops:
  0.6 1.9 %shard_map.104 = bf16[2112,128]{1,0:T(8,128)(2,1)} custom-call(bf16[64,4096]{1,0:T(8,128)(2,1)} %bitcast.30), custom_call_target="tpu_custom_call" | custom-call | bytes 1048576 | tf_op jit(solution)/shard_map/pallas_call | solution.py:115
  2.6 17.0 %all-to-all-start = ((bf16[12,176,128]{2,1,0:T(8,128)(2,1)}), bf16[12,176,128]{2,1,0:T(8,128)(2,1)}, u32[]{:S(2)}, u32[]{:S(2)}) async-start(bf16[12,176,128]{2,1,0:T(8,128)(2,1)} %bitcast.28), calls=%async_computation | async-start | bytes 1081344 | tf_op jit(solution)/shard_map/all_to_all | solution.py:235
  19.6 1.4 copy.15
  21.0 0.4 copy.14
  21.4 1.9 pad_maximum_fusion.refs_0_
  23.3 5.1 %collective-permute-start.1 = (bf16[3,4096,128]{2,1,0:T(8,128)(2,1)S(1)}, bf16[3,4096,128]{2,1,0:T(8,128)(2,1)}, u32[]{:S(2)}, u32[]{:S(2)}) collective-permute-start(bf16[3,4096,128]{2,1,0:T(8,128)(2,1)S(1)} %pad_maximum_fusion.refs_0_), channel_id=1, source_target_pairs={{0,2},{1,15},{2,0},{3,5},{4,6},{5,3},{6,4},{7,9},{8,10},{9,7},{10,... | collective-permute-start | bytes 9437192 | tf_op jit(solution)/shard_map/ppermute | solution.py:230
  28.4 8.7 %all-to-all-done = bf16[12,176,128]{2,1,0:T(8,128)(2,1)} async-done(((bf16[12,176,128]{2,1,0:T(8,128)(2,1)}), bf16[12,176,128]{2,1,0:T(8,128)(2,1)}, u32[]{:S(2)}, u32[]{:S(2)}) %all-to-all-start) | async-done | bytes 540704 | tf_op jit(solution)/shard_map/all_to_all | solution.py:235
  37.2 1.1 convert_reduce_fusion
  38.3 0.9 broadcast_in_dim.7
  39.2 8.4 %all-to-all-start.1 = ((bf16[12,176,128]{2,1,0:T(8,128)(2,1)}), bf16[12,176,128]{2,1,0:T(8,128)(2,1)}, u32[]{:S(2)}, u32[]{:S(2)}) async-start(bf16[12,176,128]{2,1,0:T(8,128)(2,1)} %broadcast_in_dim.7), calls=%async_computation.1 | async-start | bytes 1081344 | tf_op jit(solution)/shard_map/all_to_all | solution.py:238
  47.8 0.1 eq.15
  47.9 0.2 fusion
  48.1 0.1 convert_element_type.32
  48.4 0.6 add_bitcast_fusion.slots_ref
  49.0 11.0 %all-to-all-done.1 = bf16[12,176,128]{2,1,0:T(8,128)(2,1)} async-done(((bf16[12,176,128]{2,1,0:T(8,128)(2,1)}), bf16[12,176,128]{2,1,0:T(8,128)(2,1)}, u32[]{:S(2)}, u32[]{:S(2)}) %all-to-all-start.1) | async-done | bytes 540704 | tf_op jit(solution)/shard_map/all_to_all | solution.py:238
  60.0 3.2 %shard_map.105 = (bf16[64,4096]{1,0:T(8,128)(2,1)}, bf16[64,192]{1,0:T(8,128)(2,1)}, bf16[384,128]{1,0:T(8,128)(2,1)}) custom-call(bf16[2112,128]{1,0:T(8,128)(2,1)} %bitcast.3.parts_ref, bf16[192,4096]{1,0:T(8,128)(2,1)} %context_ref.1, bf16[64,192]{1,0:T(8,128)(2,1)} %bitcast.35, s32[2,192]{1,0:T(2,128)} %add_bitcast_fusion.slots_ref), custom_call_target="tpu_custom_call" | custom-call | flops 100663296 | bytes 2621440 | tf_op jit(solution)/shard_map/pallas_call | solution.py:150
  63.2 5.2 %all-to-all-start.2 = ((bf16[12,32,128]{2,1,0:T(8,128)(2,1)}), bf16[12,32,128]{2,1,0:T(8,128)(2,1)S(1)}, u32[]{:S(2)}, u32[]{:S(2)}) async-start(bf16[12,32,128]{2,1,0:T(8,128)(2,1)} %bitcast.32), calls=%async_computation.2 | async-start | bytes 196608 | tf_op jit(solution)/shard_map/all_to_all | solution.py:244
  68.4 10.1 %collective-permute-start = (bf16[3,4096,128]{2,1,0:T(8,128)(2,1)S(1)}, bf16[3,4096,128]{2,1,0:T(8,128)(2,1)}, u32[]{:S(2)}, u32[]{:S(2)}) collective-permute-start(bf16[3,4096,128]{2,1,0:T(8,128)(2,1)S(1)} %pad_maximum_fusion.refs_0_), channel_id=1, source_target_pairs={{0,1},{1,0},{2,3},{3,2},{4,5},{5,4},{6,7},{7,6},{8,9},{9,8},{10,11... | collective-permute-start | bytes 9437192 | tf_op jit(solution)/shard_map/ppermute | solution.py:231
  78.5 1.9 %collective-permute-start.2 = (bf16[3,4096,128]{2,1,0:T(8,128)(2,1)}, bf16[3,4096,128]{2,1,0:T(8,128)(2,1)}, u32[]{:S(2)}, u32[]{:S(2)}) collective-permute-start(bf16[3,4096,128]{2,1,0:T(8,128)(2,1)} %collective-permute-done.1.refs_2_), channel_id=1, source_target_pairs={{0,1},{1,0},{2,3},{3,2},{4,5},{5,4},{6,7},{7,6},{8,9},{9,8},{10,11... | collective-permute-start | bytes 9437192 | tf_op jit(solution)/shard_map/ppermute | solution.py:243
  80.5 1.2 broadcast_in_dim.10
  81.8 19.7 %all-to-all-start.3 = ((bf16[64,64,128]{2,1,0:T(8,128)(2,1)}), bf16[64,64,128]{2,1,0:T(8,128)(2,1)}, u32[]{:S(2)}, u32[]{:S(2)}) async-start(bf16[64,64,128]{2,1,0:T(8,128)(2,1)} %bitcast.24), calls=%async_computation.3 | async-start | bytes 2097152 | tf_op jit(solution)/shard_map/all_to_all | solution.py:249
  101.5 0.6 reshape.54
  102.1 28.0 %all-to-all-done.3.x_ref = bf16[64,64,128]{2,1,0:T(8,128)(2,1)} async-done(((bf16[64,64,128]{2,1,0:T(8,128)(2,1)}), bf16[64,64,128]{2,1,0:T(8,128)(2,1)}, u32[]{:S(2)}, u32[]{:S(2)}) %all-to-all-start.3) | async-done | bytes 1048608 | tf_op jit(solution)/shard_map/all_to_all | solution.py:249
  130.1 7.7 %shard_map.106 = bf16[64,64,128]{2,1,0:T(8,128)(2,1)} custom-call(bf16[64,64,128]{2,1,0:T(8,128)(2,1)} %all-to-all-done.3.x_ref, f32[1,4096]{1,0:T(1,128)} %bitcast.34, bf16[3,4096,128]{2,1,0:T(8,128)(2,1)} %copy-done, bf16[3,4096,128]{2,1,0:T(8,128)(2,1)} %collective-permute-done.refs_1_, bf16[3,4096,128]{2,1,0:T(8,128)(2,1)} %collective-permute-done.1.refs_2_, ...), custom_call_target="tpu_custom_call" | custom-call | flops 1610612736 | bytes 14680064 | tf_op jit(solution)/shard_map/pallas_call | solution.py:81
  137.8 34.5 %all_to_all.30 = bf16[64,64,128]{2,1,0:T(8,128)(2,1)S(1)} all-to-all(bf16[64,64,128]{2,1,0:T(8,128)(2,1)} %shard_map.106), channel_id=1, replica_groups=mesh['branch'=12,'group'=16,'chip'=2,'core'=2] {'group','chip','core'}, dimensions={0} | all-to-all | bytes 2097152 | tf_op jit(solution)/shard_map/all_to_all | solution.py:251
  172.3 0.2 reduce_sum.41
  172.5 0.6 pad.9
  173.2 4.6 %all-to-all-start.5 = ((bf16[12,32,128]{2,1,0:T(8,128)(2,1)}), bf16[12,32,128]{2,1,0:T(8,128)(2,1)S(1)}, u32[]{:S(2)}, u32[]{:S(2)}) async-start(bf16[12,32,128]{2,1,0:T(8,128)(2,1)} %pad.9), calls=%async_computation.5 | async-start | bytes 196608 | tf_op jit(solution)/shard_map/all_to_all | solution.py:256
  177.9 0.6 divide_bitcast_fusion.weights_ref
  178.4 9.7 %all-to-all-done.5 = bf16[12,32,128]{2,1,0:T(8,128)(2,1)S(1)} async-done(((bf16[12,32,128]{2,1,0:T(8,128)(2,1)}), bf16[12,32,128]{2,1,0:T(8,128)(2,1)S(1)}, u32[]{:S(2)}, u32[]{:S(2)}) %all-to-all-start.5) | async-done | bytes 98336 | tf_op jit(solution)/shard_map/all_to_all | solution.py:256
  188.2 0.6 copy-done.1
  188.8 1.9 shard_map.107
  (22 shorter events, 0.3 us)
Async XLA Ops:
  2.6 34.6 %all-to-all-start = ((bf16[12,176,128]{2,1,0:T(8,128)(2,1)}), bf16[12,176,128]{2,1,0:T(8,128)(2,1)}, u32[]{:S(2)}, u32[]{:S(2)}) async-start(bf16[12,176,128]{2,1,0:T(8,128)(2,1)} %bitcast.28), calls=%async_computation | async-start | bytes 1081344 | tf_op jit(solution)/shard_map/all_to_all | solution.py:235
  21.4 26.2 %copy-start.3 = (s32[192,2]{0,1:T(2,128)S(1)}, s32[192,2]{0,1:T(2,128)}, u32[]{:S(2)}) copy-start(s32[192,2]{0,1:T(2,128)} %param.13) | copy-start | bytes 4612
  23.3 58.4 %copy-start = (bf16[3,4096,128]{2,1,0:T(8,128)(2,1)}, bf16[3,4096,128]{2,1,0:T(8,128)(2,1)S(1)}, u32[]{:S(2)}) copy-start(bf16[3,4096,128]{2,1,0:T(8,128)(2,1)S(1)} %pad_maximum_fusion.refs_0_) | copy-start | bytes 9437188
  23.3 55.2 %collective-permute-start.1 = (bf16[3,4096,128]{2,1,0:T(8,128)(2,1)S(1)}, bf16[3,4096,128]{2,1,0:T(8,128)(2,1)}, u32[]{:S(2)}, u32[]{:S(2)}) collective-permute-start(bf16[3,4096,128]{2,1,0:T(8,128)(2,1)S(1)} %pad_maximum_fusion.refs_0_), channel_id=1, source_target_pairs={{0,2},{1,15},{2,0},{3,5},{4,6},{5,3},{6,4},{7,9},{8,10},{9,7},{10,... | collective-permute-start | bytes 9437192 | tf_op jit(solution)/shard_map/ppermute | solution.py:230
  39.2 20.8 %all-to-all-start.1 = ((bf16[12,176,128]{2,1,0:T(8,128)(2,1)}), bf16[12,176,128]{2,1,0:T(8,128)(2,1)}, u32[]{:S(2)}, u32[]{:S(2)}) async-start(bf16[12,176,128]{2,1,0:T(8,128)(2,1)} %broadcast_in_dim.7), calls=%async_computation.1 | async-start | bytes 1081344 | tf_op jit(solution)/shard_map/all_to_all | solution.py:238
  47.9 53.6 %copy-start.2 = (bf16[4096]{0:T(1024)(128)(2,1)S(1)}, bf16[4096]{0:T(1024)(128)(2,1)}, u32[]{:S(2)}) copy-start(bf16[4096]{0:T(1024)(128)(2,1)} %param.12) | copy-start | bytes 24580
  63.2 17.3 %all-to-all-start.2 = ((bf16[12,32,128]{2,1,0:T(8,128)(2,1)}), bf16[12,32,128]{2,1,0:T(8,128)(2,1)S(1)}, u32[]{:S(2)}, u32[]{:S(2)}) async-start(bf16[12,32,128]{2,1,0:T(8,128)(2,1)} %bitcast.32), calls=%async_computation.2 | async-start | bytes 196608 | tf_op jit(solution)/shard_map/all_to_all | solution.py:244
  68.4 33.7 %collective-permute-start = (bf16[3,4096,128]{2,1,0:T(8,128)(2,1)S(1)}, bf16[3,4096,128]{2,1,0:T(8,128)(2,1)}, u32[]{:S(2)}, u32[]{:S(2)}) collective-permute-start(bf16[3,4096,128]{2,1,0:T(8,128)(2,1)S(1)} %pad_maximum_fusion.refs_0_), channel_id=1, source_target_pairs={{0,1},{1,0},{2,3},{3,2},{4,5},{5,4},{6,7},{7,6},{8,9},{9,8},{10,11... | collective-permute-start | bytes 9437192 | tf_op jit(solution)/shard_map/ppermute | solution.py:231
  78.5 23.6 %collective-permute-start.2 = (bf16[3,4096,128]{2,1,0:T(8,128)(2,1)}, bf16[3,4096,128]{2,1,0:T(8,128)(2,1)}, u32[]{:S(2)}, u32[]{:S(2)}) collective-permute-start(bf16[3,4096,128]{2,1,0:T(8,128)(2,1)} %collective-permute-done.1.refs_2_), channel_id=1, source_target_pairs={{0,1},{1,0},{2,3},{3,2},{4,5},{5,4},{6,7},{7,6},{8,9},{9,8},{10,11... | collective-permute-start | bytes 9437192 | tf_op jit(solution)/shard_map/ppermute | solution.py:243
  81.8 48.3 %all-to-all-start.3 = ((bf16[64,64,128]{2,1,0:T(8,128)(2,1)}), bf16[64,64,128]{2,1,0:T(8,128)(2,1)}, u32[]{:S(2)}, u32[]{:S(2)}) async-start(bf16[64,64,128]{2,1,0:T(8,128)(2,1)} %bitcast.24), calls=%async_computation.3 | async-start | bytes 2097152 | tf_op jit(solution)/shard_map/all_to_all | solution.py:249
  137.8 40.0 %copy-start.4 = (s32[192,2]{0,1:T(2,128)S(1)}, s32[192,2]{0,1:T(2,128)}, u32[]{:S(2)}) copy-start(s32[192,2]{0,1:T(2,128)} %param.14) | copy-start | bytes 4612
  173.2 15.0 %all-to-all-start.5 = ((bf16[12,32,128]{2,1,0:T(8,128)(2,1)}), bf16[12,32,128]{2,1,0:T(8,128)(2,1)S(1)}, u32[]{:S(2)}, u32[]{:S(2)}) async-start(bf16[12,32,128]{2,1,0:T(8,128)(2,1)} %pad.9), calls=%async_computation.5 | async-start | bytes 196608 | tf_op jit(solution)/shard_map/all_to_all | solution.py:256
  188.2 0.6 copy-start.1

commit v4 on v2

--- a/solution.py
+++ b/solution.py
@@ -9,6 +9,7 @@
 
 epsilon = 1e-05
 MEMBERS = 4
+OUT_PARTS = 4
 ROWS = 16
 SLOT_ROWS = 32
 RING = 8
@@ -19,7 +20,7 @@
 
 
 def expert_kernel(x_ref, gain_ref, *refs):
-    given, out_ref, rows_ref, weights, sems = refs[:MEMBERS], *refs[MEMBERS:]
+    given, (out_any, out_ref, rows_ref, weights, sems, out_sems) = refs[:MEMBERS], refs[MEMBERS:]
 
     def fetch(m, kind):
         return pltpu.make_async_copy(given[m].at[kind], weights.at[m, kind], sems.at[m, kind])
@@ -27,8 +28,6 @@
     for m in range(MEMBERS):
         fetch(m, 0).start()
         fetch(m, 1).start()
-    for m in range(MEMBERS):
-        fetch(m, 2).start()
     sources, half, _ = x_ref.shape
     width = rows_ref.shape[1]
     low = lax.broadcasted_iota(jnp.int32, (half, LANES), 1) < LANES // 2
@@ -41,6 +40,8 @@
         squares[1] += bottom * bottom
         rows_ref[:half, q * LANES : (q + 1) * LANES] = top.astype(BF16)
         rows_ref[half:, q * LANES : (q + 1) * LANES] = bottom.astype(BF16)
+    for m in range(MEMBERS):
+        fetch(m, 2).start()
     total = jnp.sum(jnp.concatenate(squares, axis=0), axis=1, keepdims=True)
     inverse = lax.rsqrt(total / width + epsilon)
     chunk = 2 * LANES
@@ -60,6 +61,8 @@
     inner = jnp.concatenate(inner, axis=1)
     for m in range(MEMBERS):
         fetch(m, 2).wait()
+    leaving = []
+    span = sources // OUT_PARTS
     for q in range(0, width // LANES, 2):
         columns = [
             jnp.concatenate([weights[m, 2, (q + j) * LANES : (q + j + 1) * LANES, :] for m in range(MEMBERS)], axis=0)
@@ -72,6 +75,13 @@
             bottom = part[half:, j * LANES : (j + 1) * LANES]
             out_ref[s] = jnp.where(low, top, pltpu.roll(bottom, LANES // 2, 1)).astype(BF16)
             out_ref[s + 1] = jnp.where(low, pltpu.roll(top, LANES // 2, 1), bottom).astype(BF16)
+        if (2 * q + 4) % span == 0:
+            part = len(leaving)
+            block = pl.ds(part * span, span)
+            leaving.append(pltpu.make_async_copy(out_ref.at[block], out_any.at[block], out_sems.at[part]))
+            leaving[-1].start()
+    for copy in leaving:
+        copy.wait()
 
 
 def run_expert(x, gain, weights):
@@ -82,11 +92,13 @@
         expert_kernel,
         out_shape=jax.ShapeDtypeStruct(x.shape, BF16),
         in_specs=[pl.BlockSpec(memory_space=pltpu.VMEM)] * 2 + [pl.BlockSpec(memory_space=pl.ANY)] * MEMBERS,
-        out_specs=pl.BlockSpec(memory_space=pltpu.VMEM),
+        out_specs=pl.BlockSpec(memory_space=pl.ANY),
         scratch_shapes=[
+            pltpu.VMEM(x.shape, BF16),
             pltpu.VMEM((2 * half, width), BF16),
             pltpu.VMEM((MEMBERS,) + weights[0].shape, BF16),
             pltpu.SemaphoreType.DMA((MEMBERS, 3)),
+            pltpu.SemaphoreType.DMA((OUT_PARTS,)),
         ],
         compiler_params=pltpu.CompilerParams(vmem_limit_bytes=56 * 1024 * 1024),
         cost_estimate=pl.CostEstimate(

time: 190 us -> 190 us (level)
  no operation moved by 1% of the time
where the time goes in v4:
time: 190 us; the launch traced here: 189 us
  waiting for transfers between devices  86 us (45%)
  starting transfers between devices  77.9 us (41%)
  Pallas kernels  12.6 us (7%)
  local copies, waits for them, and re-layouts  5.3 us (3%)
  other arithmetic  5.13 us (3%)
    all_to_all x1, waiting for transfers between devices, local(): exchanged = lax.all_to_all(partial_out, SHARD, 0, 0, tiled=True)  28.6 us
    all_to_all x1, waiting for transfers between devices, local(): gathered = lax.all_to_all(copies, SHARD, 0, 0, tiled=True)  28 us
    all_to_all x1, starting transfers between devices, local(): gathered = lax.all_to_all(copies, SHARD, 0, 0, tiled=True)  19.7 us
    all_to_all x1, starting transfers between devices, local(): parts = lax.all_to_all(tiles, 'branch', 0, 0, tiled=True)  17 us
    all_to_all x1, waiting for transfers between devices, local(): lax.all_to_all(spread, 'branch', 0, 0, tiled=True)  11 us
    ppermute x1, starting transfers between devices, local(): own_core = lax.ppermute(own, 'core', [(0, 1), (1, 0)])  10.1 us
    all_to_all x1, waiting for transfers between devices, local(): returned = lax.all_to_all(expert_out, 'branch', 0, 0, tiled=True)  9.71 us
    all_to_all x1, waiting for transfers between devices, local(): parts = lax.all_to_all(tiles, 'branch', 0, 0, tiled=True)  8.73 us
  transfers between devices with their start and end apart: 9, of which 5 were waited for; matrix products, arithmetic and copies ran while one was open for 5% of the time, Pallas kernels for 2%

profile of v4, /device:TPU:1, one launch (start us, length us, event | category | flops | bytes accessed | tf_op | source)
XLA Modules:
  0.0 188.7 jit_solution(5538416636867242910)
XLA Ops:
  0.6 1.9 %shard_map.104 = bf16[2112,128]{1,0:T(8,128)(2,1)} custom-call(bf16[64,4096]{1,0:T(8,128)(2,1)} %bitcast.36), custom_call_target="tpu_custom_call" | custom-call | bytes 1048576 | tf_op jit(solution)/shard_map/pallas_call | solution.py:127
  2.6 17.0 %all-to-all-start = ((bf16[12,176,128]{2,1,0:T(8,128)(2,1)}), bf16[12,176,128]{2,1,0:T(8,128)(2,1)}, u32[]{:S(2)}, u32[]{:S(2)}) async-start(bf16[12,176,128]{2,1,0:T(8,128)(2,1)} %bitcast.34), calls=%async_computation | async-start | bytes 1081344 | tf_op jit(solution)/shard_map/all_to_all | solution.py:217
  19.5 1.4 copy.16
  21.0 0.4 copy.14
  21.4 1.9 pad_maximum_fusion.refs_0_
  23.3 5.1 %collective-permute-start = (bf16[3,4096,128]{2,1,0:T(8,128)(2,1)S(1)}, bf16[3,4096,128]{2,1,0:T(8,128)(2,1)}, u32[]{:S(2)}, u32[]{:S(2)}) collective-permute-start(bf16[3,4096,128]{2,1,0:T(8,128)(2,1)S(1)} %pad_maximum_fusion.refs_0_), channel_id=1, source_target_pairs={{0,2},{1,15},{2,0},{3,5},{4,6},{5,3},{6,4},{7,9},{8,10},{9,7},{10,... | collective-permute-start | bytes 9437192 | tf_op jit(solution)/shard_map/ppermute | solution.py:212
  28.4 8.7 %all-to-all-done = bf16[12,176,128]{2,1,0:T(8,128)(2,1)} async-done(((bf16[12,176,128]{2,1,0:T(8,128)(2,1)}), bf16[12,176,128]{2,1,0:T(8,128)(2,1)}, u32[]{:S(2)}, u32[]{:S(2)}) %all-to-all-start) | async-done | bytes 540704 | tf_op jit(solution)/shard_map/all_to_all | solution.py:217
  37.2 1.1 convert_reduce_fusion
  38.3 0.9 broadcast_in_dim.7
  39.2 8.4 %all-to-all-start.1 = ((bf16[12,176,128]{2,1,0:T(8,128)(2,1)}), bf16[12,176,128]{2,1,0:T(8,128)(2,1)}, u32[]{:S(2)}, u32[]{:S(2)}) async-start(bf16[12,176,128]{2,1,0:T(8,128)(2,1)} %broadcast_in_dim.7), calls=%async_computation.1 | async-start | bytes 1081344 | tf_op jit(solution)/shard_map/all_to_all | solution.py:220
  47.8 0.1 eq.45
  47.9 0.2 fusion.1
  48.3 0.6 multiply_add_fusion
  49.0 11.0 %all-to-all-done.1 = bf16[12,176,128]{2,1,0:T(8,128)(2,1)} async-done(((bf16[12,176,128]{2,1,0:T(8,128)(2,1)}), bf16[12,176,128]{2,1,0:T(8,128)(2,1)}, u32[]{:S(2)}, u32[]{:S(2)}) %all-to-all-start.1) | async-done | bytes 540704 | tf_op jit(solution)/shard_map/all_to_all | solution.py:220
  59.9 3.2 %shard_map.105 = (bf16[64,4096]{1,0:T(8,128)(2,1)}, bf16[64,192]{1,0:T(8,128)(2,1)}, bf16[384,128]{1,0:T(8,128)(2,1)}) custom-call(bf16[2112,128]{1,0:T(8,128)(2,1)} %bitcast.3.parts_ref, bf16[192,4096]{1,0:T(8,128)(2,1)} %context_ref.1, bf16[64,192]{1,0:T(8,128)(2,1)} %bitcast.40, s32[2,192]{1,0:T(2,128)} %bitcast.42), custom_call_target="tpu_custom_call" | custom-call | flops 100663296 | bytes 2621440 | tf_op jit(solution)/shard_map/pallas_call | solution.py:162
  63.2 5.2 %all-to-all-start.2 = ((bf16[12,32,128]{2,1,0:T(8,128)(2,1)}), bf16[12,32,128]{2,1,0:T(8,128)(2,1)S(1)}, u32[]{:S(2)}, u32[]{:S(2)}) async-start(bf16[12,32,128]{2,1,0:T(8,128)(2,1)} %bitcast.38), calls=%async_computation.2 | async-start | bytes 196608 | tf_op jit(solution)/shard_map/all_to_all | solution.py:227
  68.4 10.1 %collective-permute-start.1 = (bf16[3,4096,128]{2,1,0:T(8,128)(2,1)S(1)}, bf16[3,4096,128]{2,1,0:T(8,128)(2,1)}, u32[]{:S(2)}, u32[]{:S(2)}) collective-permute-start(bf16[3,4096,128]{2,1,0:T(8,128)(2,1)S(1)} %pad_maximum_fusion.refs_0_), channel_id=1, source_target_pairs={{0,1},{1,0},{2,3},{3,2},{4,5},{5,4},{6,7},{7,6},{8,9},{9,8},{10,11... | collective-permute-start | bytes 9437192 | tf_op jit(solution)/shard_map/ppermute | solution.py:213
  78.5 1.9 %collective-permute-start.2 = (bf16[3,4096,128]{2,1,0:T(8,128)(2,1)}, bf16[3,4096,128]{2,1,0:T(8,128)(2,1)}, u32[]{:S(2)}, u32[]{:S(2)}) collective-permute-start(bf16[3,4096,128]{2,1,0:T(8,128)(2,1)} %collective-permute-done.refs_2_), channel_id=1, source_target_pairs={{0,1},{1,0},{2,3},{3,2},{4,5},{5,4},{6,7},{7,6},{8,9},{9,8},{10,11... | collective-permute-start | bytes 9437192 | tf_op jit(solution)/shard_map/ppermute | solution.py:226
  80.5 1.2 broadcast_in_dim.10
  81.8 19.7 %all-to-all-start.3 = ((bf16[64,64,128]{2,1,0:T(8,128)(2,1)}), bf16[64,64,128]{2,1,0:T(8,128)(2,1)}, u32[]{:S(2)}, u32[]{:S(2)}) async-start(bf16[64,64,128]{2,1,0:T(8,128)(2,1)} %bitcast.31), calls=%async_computation.3 | async-start | bytes 2097152 | tf_op jit(solution)/shard_map/all_to_all | solution.py:232
  101.5 0.6 reshape.54
  102.1 28.0 %all-to-all-done.3.x_ref = bf16[64,64,128]{2,1,0:T(8,128)(2,1)} async-done(((bf16[64,64,128]{2,1,0:T(8,128)(2,1)}), bf16[64,64,128]{2,1,0:T(8,128)(2,1)}, u32[]{:S(2)}, u32[]{:S(2)}) %all-to-all-start.3) | async-done | bytes 1048608 | tf_op jit(solution)/shard_map/all_to_all | solution.py:232
  130.1 7.5 %shard_map.106 = bf16[64,64,128]{2,1,0:T(8,128)(2,1)} custom-call(bf16[64,64,128]{2,1,0:T(8,128)(2,1)} %all-to-all-done.3.x_ref, f32[1,4096]{1,0:T(1,128)} %bitcast.39, bf16[3,4096,128]{2,1,0:T(8,128)(2,1)} %copy-done, bf16[3,4096,128]{2,1,0:T(8,128)(2,1)} %collective-permute-done.1.refs_1_, bf16[3,4096,128]{2,1,0:T(8,128)(2,1)} %collective-permute-done.refs_2_, ...), custom_call_target="tpu_custom_call" | custom-call | flops 1610612736 | bytes 14680064 | tf_op jit(solution)/shard_map/pallas_call | solution.py:91
  137.6 5.9 %all-to-all-start.4 = ((bf16[64,64,128]{2,1,0:T(8,128)(2,1)}), bf16[64,64,128]{2,1,0:T(8,128)(2,1)S(1)}, u32[]{:S(2)}, u32[]{:S(2)}) async-start(bf16[64,64,128]{2,1,0:T(8,128)(2,1)} %shard_map.106), calls=%async_computation.4 | async-start | bytes 2097152 | tf_op jit(solution)/shard_map/all_to_all | solution.py:234
  143.5 28.6 %all-to-all-done.4 = bf16[64,64,128]{2,1,0:T(8,128)(2,1)S(1)} async-done(((bf16[64,64,128]{2,1,0:T(8,128)(2,1)}), bf16[64,64,128]{2,1,0:T(8,128)(2,1)S(1)}, u32[]{:S(2)}, u32[]{:S(2)}) %all-to-all-start.4) | async-done | bytes 1048608 | tf_op jit(solution)/shard_map/all_to_all | solution.py:234
  172.1 0.2 reduce_sum.41
  172.3 0.6 reshape.52
  172.9 4.6 %all-to-all-start.5 = ((bf16[12,20,128]{2,1,0:T(8,128)(2,1)}), bf16[12,20,128]{2,1,0:T(8,128)(2,1)S(1)}, u32[]{:S(2)}, u32[]{:S(2)}) async-start(bf16[12,20,128]{2,1,0:T(8,128)(2,1)} %reshape.52), calls=%async_computation.5 | async-start | bytes 147456 | tf_op jit(solution)/shard_map/all_to_all | solution.py:238
  177.6 9.7 %all-to-all-done.5 = bf16[12,20,128]{2,1,0:T(8,128)(2,1)S(1)} async-done(((bf16[12,20,128]{2,1,0:T(8,128)(2,1)}), bf16[12,20,128]{2,1,0:T(8,128)(2,1)S(1)}, u32[]{:S(2)}, u32[]{:S(2)}) %all-to-all-start.5) | async-done | bytes 61472 | tf_op jit(solution)/shard_map/all_to_all | solution.py:238
  187.5 0.3 convolution_multiply_fusion.1
  187.8 0.3 fusion
  188.1 0.6 add_convert_fusion
  (32 shorter events, 0.7 us)
Async XLA Ops:
  2.6 34.6 %all-to-all-start = ((bf16[12,176,128]{2,1,0:T(8,128)(2,1)}), bf16[12,176,128]{2,1,0:T(8,128)(2,1)}, u32[]{:S(2)}, u32[]{:S(2)}) async-start(bf16[12,176,128]{2,1,0:T(8,128)(2,1)} %bitcast.34), calls=%async_computation | async-start | bytes 1081344 | tf_op jit(solution)/shard_map/all_to_all | solution.py:217
  21.4 26.2 %copy-start.4 = (s32[192,2]{0,1:T(2,128)S(1)}, s32[192,2]{0,1:T(2,128)}, u32[]{:S(2)}) copy-start(s32[192,2]{0,1:T(2,128)} %param.13) | copy-start | bytes 4612
  23.3 58.4 %copy-start = (bf16[3,4096,128]{2,1,0:T(8,128)(2,1)}, bf16[3,4096,128]{2,1,0:T(8,128)(2,1)S(1)}, u32[]{:S(2)}) copy-start(bf16[3,4096,128]{2,1,0:T(8,128)(2,1)S(1)} %pad_maximum_fusion.refs_0_) | copy-start | bytes 9437188
  23.3 55.2 %collective-permute-start = (bf16[3,4096,128]{2,1,0:T(8,128)(2,1)S(1)}, bf16[3,4096,128]{2,1,0:T(8,128)(2,1)}, u32[]{:S(2)}, u32[]{:S(2)}) collective-permute-start(bf16[3,4096,128]{2,1,0:T(8,128)(2,1)S(1)} %pad_maximum_fusion.refs_0_), channel_id=1, source_target_pairs={{0,2},{1,15},{2,0},{3,5},{4,6},{5,3},{6,4},{7,9},{8,10},{9,7},{10,... | collective-permute-start | bytes 9437192 | tf_op jit(solution)/shard_map/ppermute | solution.py:212
  39.2 20.8 %all-to-all-start.1 = ((bf16[12,176,128]{2,1,0:T(8,128)(2,1)}), bf16[12,176,128]{2,1,0:T(8,128)(2,1)}, u32[]{:S(2)}, u32[]{:S(2)}) async-start(bf16[12,176,128]{2,1,0:T(8,128)(2,1)} %broadcast_in_dim.7), calls=%async_computation.1 | async-start | bytes 1081344 | tf_op jit(solution)/shard_map/all_to_all | solution.py:220
  47.9 53.6 %copy-start.3 = (bf16[4096]{0:T(1024)(128)(2,1)S(1)}, bf16[4096]{0:T(1024)(128)(2,1)}, u32[]{:S(2)}) copy-start(bf16[4096]{0:T(1024)(128)(2,1)} %param.12) | copy-start | bytes 24580
  63.2 17.3 %all-to-all-start.2 = ((bf16[12,32,128]{2,1,0:T(8,128)(2,1)}), bf16[12,32,128]{2,1,0:T(8,128)(2,1)S(1)}, u32[]{:S(2)}, u32[]{:S(2)}) async-start(bf16[12,32,128]{2,1,0:T(8,128)(2,1)} %bitcast.38), calls=%async_computation.2 | async-start | bytes 196608 | tf_op jit(solution)/shard_map/all_to_all | solution.py:227
  68.4 33.7 %collective-permute-start.1 = (bf16[3,4096,128]{2,1,0:T(8,128)(2,1)S(1)}, bf16[3,4096,128]{2,1,0:T(8,128)(2,1)}, u32[]{:S(2)}, u32[]{:S(2)}) collective-permute-start(bf16[3,4096,128]{2,1,0:T(8,128)(2,1)S(1)} %pad_maximum_fusion.refs_0_), channel_id=1, source_target_pairs={{0,1},{1,0},{2,3},{3,2},{4,5},{5,4},{6,7},{7,6},{8,9},{9,8},{10,11... | collective-permute-start | bytes 9437192 | tf_op jit(solution)/shard_map/ppermute | solution.py:213
  78.5 23.6 %collective-permute-start.2 = (bf16[3,4096,128]{2,1,0:T(8,128)(2,1)}, bf16[3,4096,128]{2,1,0:T(8,128)(2,1)}, u32[]{:S(2)}, u32[]{:S(2)}) collective-permute-start(bf16[3,4096,128]{2,1,0:T(8,128)(2,1)} %collective-permute-done.refs_2_), channel_id=1, source_target_pairs={{0,1},{1,0},{2,3},{3,2},{4,5},{5,4},{6,7},{7,6},{8,9},{9,8},{10,11... | collective-permute-start | bytes 9437192 | tf_op jit(solution)/shard_map/ppermute | solution.py:226
  81.8 48.3 %all-to-all-start.3 = ((bf16[64,64,128]{2,1,0:T(8,128)(2,1)}), bf16[64,64,128]{2,1,0:T(8,128)(2,1)}, u32[]{:S(2)}, u32[]{:S(2)}) async-start(bf16[64,64,128]{2,1,0:T(8,128)(2,1)} %bitcast.31), calls=%async_computation.3 | async-start | bytes 2097152 | tf_op jit(solution)/shard_map/all_to_all | solution.py:232
  130.1 13.4 %copy-start.5 = (s32[192,2]{0,1:T(2,128)S(1)}, s32[192,2]{0,1:T(2,128)}, u32[]{:S(2)}) copy-start(s32[192,2]{0,1:T(2,128)} %param.14) | copy-start | bytes 4612
  130.1 13.4 %copy-start.2 = (s32[192,2]{0,1:T(2,128)S(1)}, s32[192,2]{0,1:T(2,128)}, u32[]{:S(2)}) copy-start(s32[192,2]{0,1:T(2,128)} %multiply_add_fusion) | copy-start | bytes 4612
  137.6 50.5 %copy-start.1 = (bf16[64,192]{1,0:T(8,128)(2,1)S(1)}, bf16[64,192]{1,0:T(8,128)(2,1)}, u32[]{:S(2)}) copy-start(bf16[64,192]{1,0:T(8,128)(2,1)} %get-tuple-element.7) | copy-start | bytes 73732
  137.6 34.5 %all-to-all-start.4 = ((bf16[64,64,128]{2,1,0:T(8,128)(2,1)}), bf16[64,64,128]{2,1,0:T(8,128)(2,1)S(1)}, u32[]{:S(2)}, u32[]{:S(2)}) async-start(bf16[64,64,128]{2,1,0:T(8,128)(2,1)} %shard_map.106), calls=%async_computation.4 | async-start | bytes 2097152 | tf_op jit(solution)/shard_map/all_to_all | solution.py:234
  172.9 14.4 %all-to-all-start.5 = ((bf16[12,20,128]{2,1,0:T(8,128)(2,1)}), bf16[12,20,128]{2,1,0:T(8,128)(2,1)S(1)}, u32[]{:S(2)}, u32[]{:S(2)}) async-start(bf16[12,20,128]{2,1,0:T(8,128)(2,1)} %reshape.52), calls=%async_computation.5 | async-start | bytes 147456 | tf_op jit(solution)/shard_map/all_to_all | solution.py:238
